TPU v7x, 256 devices: a whole 4x4x8 slice. The times are simulated.
256 devices in a mesh: seq: 64 (over z, x, core), ch: 4 (over y).
Axes of the slice: x: 4, y: 4, z: 8, core: 2. Of those that a mesh axis runs over, the one named last changes fastest.
Arguments:
- tokens: bfloat16 [16384, 4096], P('seq', 'ch'), may hold values from -6 to 6
- w_value: bfloat16 [4096, 2048], P(None, 'ch'), may hold values from -0.09375 to 0.09375
- w_gate: bfloat16 [4096, 2048], P(None, 'ch'), may hold values from -0.09375 to 0.09375
- short_value: float32 [3, 2048], P(None, 'ch'), may hold values from -3.5 to 3.5
- short_gate: float32 [3, 2048], P(None, 'ch'), may hold values from -3.5 to 3.5
- skip_bias: float32 [2048], P('ch'), may hold values from 0.5 to 1.5
- long_filter: float32 [16384, 2048], P('seq', 'ch'), may hold values from -0.046875 to 0.046875
- grad_out: bfloat16 [16384, 2048], P('seq', 'ch'), may hold values from -0.046875 to 0.046875
Outputs:
- output: bfloat16 [16384, 2048], P('seq', 'ch')
- filter_grad: float32 [16384, 2048], P('seq', 'ch')
All inputs are finite; a program needn't handle non-finite values.
Results may differ from a plain program's by a relative error of at most 0.0095.
Values may be sent and summed in bfloat16 or wider, within the bound.
A program may use at most 128 MiB of HBM per device.

v0:
```python
import math

import jax
import jax.numpy as jnp
from jax import lax
from jax.sharding import PartitionSpec as P

best_precision = lax.Precision.HIGHEST


def shortened(value):

    def short(part):
        return part.astype(jnp.bfloat16) if part.dtype == jnp.float32 else part

    return jax.tree.map(short, value)


def from_behind(value, axis, steps):
    count = lax.axis_size(axis)
    initial, last = (max(0, -steps), min(count, count - steps))
    return lax.ppermute(value, axis, [(source, source + steps) for source in range(initial, last)])


def counting(length):
    return jnp.arange(length, dtype=jnp.int32)


def phase_table(left_index, right_index, modulus):
    turns = left_index[:, None] * right_index[None, :] % modulus
    angle = turns.astype(jnp.float32) * (2.0 * math.pi / modulus)
    return (jnp.cos(angle), jnp.sin(angle))


def apply_table(form, table, signal):
    return jnp.einsum(form, table, signal, precision=best_precision)


def cross_whole(signal):
    axis_count = signal.shape[1]
    cos_table, sin_table = phase_table(
        counting(2 * axis_count), counting(axis_count), 2 * axis_count
    )
    real_part = apply_table("km,amgi->akgi", cos_table, signal)
    imag_part = -apply_table("km,amgi->akgi", sin_table, signal)
    return (real_part, imag_part)


def slot_numbers(own_index):
    slots = 2 * own_index + counting(2)
    return slots


def forward(signals):
    row_count = signals.shape[1]
    axis_count = lax.axis_size("seq")
    own_index = lax.axis_index("seq")
    length = 2 * row_count * axis_count
    slots = slot_numbers(own_index)
    shaped = signals[:, None]
    first_real, first_imag = cross_whole(
        lax.all_to_all(shaped, "seq", split_axis=2, concat_axis=1, tiled=True)
    )
    real_part = lax.all_to_all(first_real, "seq", split_axis=1, concat_axis=2, tiled=True)
    imag_part = lax.all_to_all(first_imag, "seq", split_axis=1, concat_axis=2, tiled=True)
    real_part, imag_part = (real_part, imag_part)
    twist_cos, twist_sin = phase_table(slots, counting(row_count), length)
    twist_cos = twist_cos[None, :, :, None]
    twist_sin = twist_sin[None, :, :, None]
    turned_real = real_part * twist_cos + imag_part * twist_sin
    turned_imag = imag_part * twist_cos - real_part * twist_sin
    cos_table, sin_table = phase_table(counting(row_count), counting(row_count), row_count)
    out_real = apply_table("kn,asni->aski", cos_table, turned_real) + apply_table(
        "kn,asni->aski", sin_table, turned_imag
    )
    out_imag = apply_table("kn,asni->aski", cos_table, turned_imag) - apply_table(
        "kn,asni->aski", sin_table, turned_real
    )
    spectra = (out_real, out_imag)
    return (spectra, slots)


def inverse(spec_real, spec_imag, slots):
    row_count = spec_real.shape[2]
    axis_count = lax.axis_size("seq")
    length = 2 * row_count * axis_count
    cos_table, sin_table = phase_table(counting(row_count), counting(row_count), row_count)
    back_real = apply_table("nk,bski->bsni", cos_table, spec_real) - apply_table(
        "nk,bski->bsni", sin_table, spec_imag
    )
    back_imag = apply_table("nk,bski->bsni", cos_table, spec_imag) + apply_table(
        "nk,bski->bsni", sin_table, spec_real
    )
    twist_cos, twist_sin = phase_table(slots, counting(row_count), length)
    twist_cos = twist_cos[None, :, :, None]
    twist_sin = twist_sin[None, :, :, None]
    turned_real = back_real * twist_cos - back_imag * twist_sin
    turned_imag = back_real * twist_sin + back_imag * twist_cos
    real_part = lax.all_to_all(
        turned_real.astype(jnp.bfloat16), "seq", split_axis=2, concat_axis=1, tiled=True
    ).astype(turned_real.dtype)
    imag_part = lax.all_to_all(
        turned_imag.astype(jnp.bfloat16), "seq", split_axis=2, concat_axis=1, tiled=True
    ).astype(turned_imag.dtype)
    cos_rows, sin_rows = phase_table(counting(axis_count), counting(2 * axis_count), 2 * axis_count)
    summed = apply_table("mk,bkgi->bmgi", cos_rows, real_part) - apply_table(
        "mk,bkgi->bmgi", sin_rows, imag_part
    )
    spread = summed / length
    restored = lax.all_to_all(
        shortened(spread), "seq", split_axis=1, concat_axis=2, tiled=True
    ).astype(spread.dtype)
    return restored[:, 0]


def shards(tokens, w_value, w_gate, short_value, short_gate, skip_bias, long_filter, grad_out):
    piece = lax.all_gather(tokens, "ch", axis=1, tiled=True)
    proj_value = jnp.dot(piece, w_value, preferred_element_type=jnp.float32)
    proj_gate = jnp.dot(piece, w_gate, preferred_element_type=jnp.float32)
    projected = lax.optimization_barrier(
        jnp.stack([proj_value.astype(jnp.bfloat16), proj_gate.astype(jnp.bfloat16)])
    )
    tail_rows = from_behind(projected[:, -2:], "seq", 1)
    widened = jnp.concatenate([tail_rows, projected], axis=1).astype(jnp.float32)
    kernels = jnp.stack([short_value, short_gate])
    filtered = (
        kernels[:, 0, None] * widened[:, 2:]
        + kernels[:, 1, None] * widened[:, 1:-1]
        + kernels[:, 2, None] * widened[:, :-2]
    )
    value_act = filtered[0]
    gate_act = filtered[1]
    grad_mixed = grad_out.astype(jnp.float32) * gate_act
    (first_real, first_imag), slots = forward(jnp.stack([value_act, long_filter]))
    value_real, value_imag = (first_real[:1], first_imag[:1])
    filter_real, filter_imag = (first_real[1:], first_imag[1:])
    conv_real = value_real * filter_real - value_imag * filter_imag
    conv_imag = value_real * filter_imag + value_imag * filter_real
    long_conv = inverse(conv_real, conv_imag, slots)[0]
    (grad_real, grad_imag), slots = forward(grad_mixed[None])
    corr_real = value_real * grad_real + value_imag * grad_imag
    corr_imag = value_real * grad_imag - value_imag * grad_real
    filter_grad = inverse(corr_real, corr_imag, slots)[0]
    mixed_sum = long_conv + skip_bias * value_act
    return ((gate_act * mixed_sum).astype(jnp.bfloat16), filter_grad)


def solution(mesh):
    return jax.shard_map(
        shards,
        mesh=mesh,
        in_specs=(
            P("seq", "ch"),
            P(None, "ch"),
            P(None, "ch"),
            P(None, "ch"),
            P(None, "ch"),
            P("ch"),
            P("seq", "ch"),
            P("seq", "ch"),
        ),
        out_specs=(P("seq", "ch"), P("seq", "ch")),
        check_vma=False,
    )
```

profile of v0, /device:TPU:1, one launch (start us, length us, event | category | flops | bytes accessed | tf_op | source)
XLA Modules:
  0.0 503.5 jit_solution(8527156743916382186)
XLA Ops:
  8.7 38.3 %all-gather.2.cloned.1.call-done = bf16[256,4096]{1,0:T(8,128)(2,1)} async-done(((bf16[256,1024]{1,0:T(8,128)(2,1)}), bf16[256,4096]{1,0:T(8,128)(2,1)}) %all-gather.2.cloned.1.call-update) | async-done | bytes 2097168 | tf_op jit(solution)/shard_map/all_gather | solution.py:117
  47.1 4.2 fusion.11
  60.0 12.1 %all-to-all-start.6 = ((f32[1,1,256,512]{3,1,0,2:T(1,128)}), f32[1,1,256,512]{3,1,0,2:T(1,128)S(1)}, u32[]{:S(2)}, u32[]{:S(2)}) async-start(f32[1,1,256,512]{3,1,0,2:T(1,128)} %copy.111), calls=%async_computation.6 | async-start | bytes 1048576 | tf_op jit(solution)/shard_map/all_to_all | solution.py:62
  74.0 15.8 %all-to-all-done.6 = f32[1,1,256,512]{3,1,0,2:T(1,128)S(1)} async-done(((f32[1,1,256,512]{3,1,0,2:T(1,128)}), f32[1,1,256,512]{3,1,0,2:T(1,128)S(1)}, u32[]{:S(2)}, u32[]{:S(2)}) %all-to-all-start.6) | async-done | bytes 524320 | tf_op jit(solution)/shard_map/all_to_all | solution.py:62
  89.8 5.7 %all-to-all-start = ((f32[2,1,256,512]{3,0,1,2:T(2,128)}), f32[2,1,256,512]{3,0,1,2:T(2,128)S(1)}, u32[]{:S(2)}, u32[]{:S(2)}) async-start(f32[2,1,256,512]{3,0,1,2:T(2,128)} %copy.91), calls=%async_computation | async-start | bytes 2097152 | tf_op jit(solution)/shard_map/all_to_all | solution.py:62
  102.5 21.1 %all-to-all-done = f32[2,1,256,512]{3,0,1,2:T(2,128)S(1)} async-done(((f32[2,1,256,512]{3,0,1,2:T(2,128)}), f32[2,1,256,512]{3,0,1,2:T(2,128)S(1)}, u32[]{:S(2)}, u32[]{:S(2)}) %all-to-all-start) | async-done | bytes 1048608 | tf_op jit(solution)/shard_map/all_to_all | solution.py:62
  123.5 7.1 %all-to-all-start.7 = ((f32[1,128,4,512]{3,2,0,1:T(4,128)}), f32[1,128,4,512]{3,2,0,1:T(4,128)}, u32[]{:S(2)}, u32[]{:S(2)}) async-start(f32[1,128,4,512]{3,2,0,1:T(4,128)} %copy.113), calls=%async_computation.7 | async-start | bytes 2097152 | tf_op jit(solution)/shard_map/all_to_all | solution.py:64
  136.1 22.2 %all-to-all-done.7 = f32[1,128,4,512]{3,2,0,1:T(4,128)} async-done(((f32[1,128,4,512]{3,2,0,1:T(4,128)}), f32[1,128,4,512]{3,2,0,1:T(4,128)}, u32[]{:S(2)}, u32[]{:S(2)}) %all-to-all-start.7) | async-done | bytes 1048608 | tf_op jit(solution)/shard_map/all_to_all | solution.py:64
  158.3 6.5 %all-to-all-start.8 = ((f32[1,128,4,512]{3,2,0,1:T(4,128)}), f32[1,128,4,512]{3,2,0,1:T(4,128)S(1)}, u32[]{:S(2)}, u32[]{:S(2)}) async-start(f32[1,128,4,512]{3,2,0,1:T(4,128)} %copy.117), calls=%async_computation.8 | async-start | bytes 2097152 | tf_op jit(solution)/shard_map/all_to_all | solution.py:65
  164.8 5.2 %convolution_bitcast_fusion = f32[2,128,4,512]{1,3,2,0:T(8,128)} fusion(f32[2,64,4,512]{3,0,2,1:T(2,128)S(1)} %bitcast.243), kind=kOutput, calls=%fused_computation.5 | convolution fusion | flops 402767872 | bytes 3145728 | tf_op jit(solution)/shard_map/km,amgi->akgi/dot_general | solution.py:36
  173.2 19.6 %all-to-all-done.8 = f32[1,128,4,512]{3,2,0,1:T(4,128)S(1)} async-done(((f32[1,128,4,512]{3,2,0,1:T(4,128)}), f32[1,128,4,512]{3,2,0,1:T(4,128)S(1)}, u32[]{:S(2)}, u32[]{:S(2)}) %all-to-all-start.8) | async-done | bytes 1048608 | tf_op jit(solution)/shard_map/all_to_all | solution.py:65
  192.8 6.7 %all-to-all-start.1 = ((f32[2,128,4,512]{3,2,0,1:T(4,128)}), f32[2,128,4,512]{3,2,0,1:T(4,128)}, u32[]{:S(2)}, u32[]{:S(2)}) async-start(f32[2,128,4,512]{3,2,0,1:T(4,128)} %copy.93), calls=%async_computation.1 | async-start | bytes 4194304 | tf_op jit(solution)/shard_map/all_to_all | solution.py:64
  199.5 5.2 %negate_bitcast_fusion = f32[2,128,4,512]{1,3,2,0:T(8,128)} fusion(f32[2,64,4,512]{3,0,2,1:T(2,128)S(1)} %bitcast.244), kind=kOutput, calls=%fused_computation.4 | convolution fusion | flops 403292160 | bytes 3145728 | tf_op jit(solution)/shard_map/km,amgi->akgi/dot_general | solution.py:36
  207.8 41.3 %all-to-all-done.1 = f32[2,128,4,512]{3,2,0,1:T(4,128)} async-done(((f32[2,128,4,512]{3,2,0,1:T(4,128)}), f32[2,128,4,512]{3,2,0,1:T(4,128)}, u32[]{:S(2)}, u32[]{:S(2)}) %all-to-all-start.1) | async-done | bytes 2097184 | tf_op jit(solution)/shard_map/all_to_all | solution.py:64
  249.1 15.9 %all-to-all-start.2 = ((f32[2,128,4,512]{3,2,0,1:T(4,128)}), f32[2,128,4,512]{3,2,0,1:T(4,128)}, u32[]{:S(2)}, u32[]{:S(2)}) async-start(f32[2,128,4,512]{3,2,0,1:T(4,128)} %copy.98), calls=%async_computation.2 | async-start | bytes 4194304 | tf_op jit(solution)/shard_map/all_to_all | solution.py:65
  283.4 30.9 %all-to-all-done.2 = f32[2,128,4,512]{3,2,0,1:T(4,128)} async-done(((f32[2,128,4,512]{3,2,0,1:T(4,128)}), f32[2,128,4,512]{3,2,0,1:T(4,128)}, u32[]{:S(2)}, u32[]{:S(2)}) %all-to-all-start.2) | async-done | bytes 2097184 | tf_op jit(solution)/shard_map/all_to_all | solution.py:65
  317.5 3.8 multiply_add_fusion
  324.1 4.1 fusion.63
  328.2 4.2 copy.103
  332.4 4.6 fusion.61
  363.2 7.1 %all-to-all-start.9 = ((bf16[1,2,256,512]{3,1,0,2:T(2,128)(2,1)}), bf16[1,2,256,512]{3,1,0,2:T(2,128)(2,1)S(1)}, u32[]{:S(2)}, u32[]{:S(2)}) async-start(bf16[1,2,256,512]{3,1,0,2:T(2,128)(2,1)} %copy.124), calls=%async_computation.9 | async-start | bytes 1048576 | tf_op jit(solution)/shard_map/all_to_all | solution.py:99
  371.5 16.5 %all-to-all-done.9 = bf16[1,2,256,512]{3,1,0,2:T(2,128)(2,1)S(1)} async-done(((bf16[1,2,256,512]{3,1,0,2:T(2,128)(2,1)}), bf16[1,2,256,512]{3,1,0,2:T(2,128)(2,1)S(1)}, u32[]{:S(2)}, u32[]{:S(2)}) %all-to-all-start.9) | async-done | bytes 524320 | tf_op jit(solution)/shard_map/all_to_all | solution.py:99
  388.0 5.7 %all-to-all-start.3 = ((bf16[1,2,256,512]{3,1,0,2:T(2,128)(2,1)}), bf16[1,2,256,512]{3,1,0,2:T(2,128)(2,1)S(1)}, u32[]{:S(2)}, u32[]{:S(2)}) async-start(bf16[1,2,256,512]{3,1,0,2:T(2,128)(2,1)} %copy.106), calls=%async_computation.3 | async-start | bytes 1048576 | tf_op jit(solution)/shard_map/all_to_all | solution.py:99
  394.9 16.5 %all-to-all-done.3 = bf16[1,2,256,512]{3,1,0,2:T(2,128)(2,1)S(1)} async-done(((bf16[1,2,256,512]{3,1,0,2:T(2,128)(2,1)}), bf16[1,2,256,512]{3,1,0,2:T(2,128)(2,1)S(1)}, u32[]{:S(2)}, u32[]{:S(2)}) %all-to-all-start.3) | async-done | bytes 524320 | tf_op jit(solution)/shard_map/all_to_all | solution.py:99
  411.4 5.7 %all-to-all-start.4 = ((bf16[1,2,256,512]{3,1,0,2:T(2,128)(2,1)}), bf16[1,2,256,512]{3,1,0,2:T(2,128)(2,1)S(1)}, u32[]{:S(2)}, u32[]{:S(2)}) async-start(bf16[1,2,256,512]{3,1,0,2:T(2,128)(2,1)} %copy.108), calls=%async_computation.4 | async-start | bytes 1048576 | tf_op jit(solution)/shard_map/all_to_all | solution.py:102
  418.3 16.5 %all-to-all-done.4 = bf16[1,2,256,512]{3,1,0,2:T(2,128)(2,1)S(1)} async-done(((bf16[1,2,256,512]{3,1,0,2:T(2,128)(2,1)}), bf16[1,2,256,512]{3,1,0,2:T(2,128)(2,1)S(1)}, u32[]{:S(2)}, u32[]{:S(2)}) %all-to-all-start.4) | async-done | bytes 524320 | tf_op jit(solution)/shard_map/all_to_all | solution.py:102
  434.9 5.7 %all-to-all-start.10 = ((bf16[1,2,256,512]{3,1,0,2:T(2,128)(2,1)}), bf16[1,2,256,512]{3,1,0,2:T(2,128)(2,1)S(1)}, u32[]{:S(2)}, u32[]{:S(2)}) async-start(bf16[1,2,256,512]{3,1,0,2:T(2,128)(2,1)} %copy.126), calls=%async_computation.10 | async-start | bytes 1048576 | tf_op jit(solution)/shard_map/all_to_all | solution.py:102
  447.3 11.0 %all-to-all-done.10 = bf16[1,2,256,512]{3,1,0,2:T(2,128)(2,1)S(1)} async-done(((bf16[1,2,256,512]{3,1,0,2:T(2,128)(2,1)}), bf16[1,2,256,512]{3,1,0,2:T(2,128)(2,1)S(1)}, u32[]{:S(2)}, u32[]{:S(2)}) %all-to-all-start.10) | async-done | bytes 524320 | tf_op jit(solution)/shard_map/all_to_all | solution.py:102
  458.3 6.1 %all-to-all-start.5 = ((bf16[1,64,4,512]{3,2,0,1:T(4,128)(2,1)}), bf16[1,64,4,512]{3,2,0,1:T(4,128)(2,1)S(1)}, u32[]{:S(2)}, u32[]{:S(2)}) async-start(bf16[1,64,4,512]{3,2,0,1:T(4,128)(2,1)} %copy.110), calls=%async_computation.5 | async-start | bytes 524288 | tf_op jit(solution)/shard_map/all_to_all | solution.py:110
  467.5 10.0 %all-to-all-done.5 = bf16[1,64,4,512]{3,2,0,1:T(4,128)(2,1)S(1)} async-done(((bf16[1,64,4,512]{3,2,0,1:T(4,128)(2,1)}), bf16[1,64,4,512]{3,2,0,1:T(4,128)(2,1)S(1)}, u32[]{:S(2)}, u32[]{:S(2)}) %all-to-all-start.5) | async-done | bytes 262176 | tf_op jit(solution)/shard_map/all_to_all | solution.py:110
  477.5 4.7 all-to-all-start.11
  483.1 12.2 %all-to-all-done.11 = bf16[1,64,4,512]{3,2,0,1:T(4,128)(2,1)S(1)} async-done(((bf16[1,64,4,512]{3,2,0,1:T(4,128)(2,1)}), bf16[1,64,4,512]{3,2,0,1:T(4,128)(2,1)S(1)}, u32[]{:S(2)}, u32[]{:S(2)}) %all-to-all-start.11) | async-done | bytes 262176 | tf_op jit(solution)/shard_map/all_to_all | solution.py:110
  (94 shorter events, 96.2 us)
Async XLA Ops:
  7.2 39.9 %all-gather.2.cloned.1.call-start = ((), (), s32[]{:S(2)}) async-start(), calls=%async_computation.12 | async-start | bytes 2621440 | tf_op jit(solution)/shard_map/all_gather | solution.py:117
  47.1 4.2 copy-start.9
  47.1 4.7 copy-start.10
  53.1 4.4 collective-permute-start
  57.6 1.0 copy-start.7
  58.6 13.6 %copy-start.6 = (f32[256,512]{1,0:T(8,128)S(1)}, f32[256,512]{1,0:T(8,128)}, u32[]{:S(2)}) copy-start(f32[256,512]{1,0:T(8,128)} %param.14) | copy-start | bytes 1572868
  60.0 29.8 %all-to-all-start.6 = ((f32[1,1,256,512]{3,1,0,2:T(1,128)}), f32[1,1,256,512]{3,1,0,2:T(1,128)S(1)}, u32[]{:S(2)}, u32[]{:S(2)}) async-start(f32[1,1,256,512]{3,1,0,2:T(1,128)} %copy.111), calls=%async_computation.6 | async-start | bytes 1048576 | tf_op jit(solution)/shard_map/all_to_all | solution.py:62
  89.8 33.7 %all-to-all-start = ((f32[2,1,256,512]{3,0,1,2:T(2,128)}), f32[2,1,256,512]{3,0,1,2:T(2,128)S(1)}, u32[]{:S(2)}, u32[]{:S(2)}) async-start(f32[2,1,256,512]{3,0,1,2:T(2,128)} %copy.91), calls=%async_computation | async-start | bytes 2097152 | tf_op jit(solution)/shard_map/all_to_all | solution.py:62
  123.5 34.8 %all-to-all-start.7 = ((f32[1,128,4,512]{3,2,0,1:T(4,128)}), f32[1,128,4,512]{3,2,0,1:T(4,128)}, u32[]{:S(2)}, u32[]{:S(2)}) async-start(f32[1,128,4,512]{3,2,0,1:T(4,128)} %copy.113), calls=%async_computation.7 | async-start | bytes 2097152 | tf_op jit(solution)/shard_map/all_to_all | solution.py:64
  158.3 34.5 %all-to-all-start.8 = ((f32[1,128,4,512]{3,2,0,1:T(4,128)}), f32[1,128,4,512]{3,2,0,1:T(4,128)S(1)}, u32[]{:S(2)}, u32[]{:S(2)}) async-start(f32[1,128,4,512]{3,2,0,1:T(4,128)} %copy.117), calls=%async_computation.8 | async-start | bytes 2097152 | tf_op jit(solution)/shard_map/all_to_all | solution.py:65
  192.8 56.3 %all-to-all-start.1 = ((f32[2,128,4,512]{3,2,0,1:T(4,128)}), f32[2,128,4,512]{3,2,0,1:T(4,128)}, u32[]{:S(2)}, u32[]{:S(2)}) async-start(f32[2,128,4,512]{3,2,0,1:T(4,128)} %copy.93), calls=%async_computation.1 | async-start | bytes 4194304 | tf_op jit(solution)/shard_map/all_to_all | solution.py:64
  249.1 65.2 %all-to-all-start.2 = ((f32[2,128,4,512]{3,2,0,1:T(4,128)}), f32[2,128,4,512]{3,2,0,1:T(4,128)}, u32[]{:S(2)}, u32[]{:S(2)}) async-start(f32[2,128,4,512]{3,2,0,1:T(4,128)} %copy.98), calls=%async_computation.2 | async-start | bytes 4194304 | tf_op jit(solution)/shard_map/all_to_all | solution.py:65
  270.4 3.8 copy-start.1
  332.4 4.6 copy-start
  332.4 4.6 copy-start.3
  339.9 3.0 copy-start.2
  339.9 3.0 copy-start.4
  339.9 3.0 copy-start.5
  363.2 24.8 %all-to-all-start.9 = ((bf16[1,2,256,512]{3,1,0,2:T(2,128)(2,1)}), bf16[1,2,256,512]{3,1,0,2:T(2,128)(2,1)S(1)}, u32[]{:S(2)}, u32[]{:S(2)}) async-start(bf16[1,2,256,512]{3,1,0,2:T(2,128)(2,1)} %copy.124), calls=%async_computation.9 | async-start | bytes 1048576 | tf_op jit(solution)/shard_map/all_to_all | solution.py:99
  388.0 23.4 %all-to-all-start.3 = ((bf16[1,2,256,512]{3,1,0,2:T(2,128)(2,1)}), bf16[1,2,256,512]{3,1,0,2:T(2,128)(2,1)S(1)}, u32[]{:S(2)}, u32[]{:S(2)}) async-start(bf16[1,2,256,512]{3,1,0,2:T(2,128)(2,1)} %copy.106), calls=%async_computation.3 | async-start | bytes 1048576 | tf_op jit(solution)/shard_map/all_to_all | solution.py:99
  411.4 23.4 %all-to-all-start.4 = ((bf16[1,2,256,512]{3,1,0,2:T(2,128)(2,1)}), bf16[1,2,256,512]{3,1,0,2:T(2,128)(2,1)S(1)}, u32[]{:S(2)}, u32[]{:S(2)}) async-start(bf16[1,2,256,512]{3,1,0,2:T(2,128)(2,1)} %copy.108), calls=%async_computation.4 | async-start | bytes 1048576 | tf_op jit(solution)/shard_map/all_to_all | solution.py:102
  434.9 23.4 %all-to-all-start.10 = ((bf16[1,2,256,512]{3,1,0,2:T(2,128)(2,1)}), bf16[1,2,256,512]{3,1,0,2:T(2,128)(2,1)S(1)}, u32[]{:S(2)}, u32[]{:S(2)}) async-start(bf16[1,2,256,512]{3,1,0,2:T(2,128)(2,1)} %copy.126), calls=%async_computation.10 | async-start | bytes 1048576 | tf_op jit(solution)/shard_map/all_to_all | solution.py:102
  458.3 19.1 %all-to-all-start.5 = ((bf16[1,64,4,512]{3,2,0,1:T(4,128)(2,1)}), bf16[1,64,4,512]{3,2,0,1:T(4,128)(2,1)S(1)}, u32[]{:S(2)}, u32[]{:S(2)}) async-start(bf16[1,64,4,512]{3,2,0,1:T(4,128)(2,1)} %copy.110), calls=%async_computation.5 | async-start | bytes 524288 | tf_op jit(solution)/shard_map/all_to_all | solution.py:110
  465.6 16.7 %copy-start.8 = (f32[512]{0:T(512)S(1)}, f32[512]{0:T(512)}, u32[]{:S(2)}) copy-start(f32[512]{0:T(512)} %param.13) | copy-start | bytes 6148
  477.5 17.9 %all-to-all-start.11 = ((bf16[1,64,4,512]{3,2,0,1:T(4,128)(2,1)}), bf16[1,64,4,512]{3,2,0,1:T(4,128)(2,1)S(1)}, u32[]{:S(2)}, u32[]{:S(2)}) async-start(bf16[1,64,4,512]{3,2,0,1:T(4,128)(2,1)} %copy.128), calls=%async_computation.11 | async-start | bytes 524288 | tf_op jit(solution)/shard_map/all_to_all | solution.py:110
Sparse Core Ops, SparseCore 0:
  9.8 37.2 all-gather.1
where the time goes:
time: 513 us; the launch traced here: 503 us
  waiting for transfers between devices  273 us (53%)
  starting transfers between devices  92.6 us (18%)
  matrix products  65.2 us (13%)
  local copies, waits for them, and re-layouts  47.6 us (9%)
  between operations  15.1 us (3%)
  other arithmetic  9.63 us (2%)
    all_to_all x2, waiting for transfers between devices, forward(): lax.all_to_all(first_real, 'seq', split_axis=1, concat_axis=2, tiled=True)  63.5 us
    dot_general x24, matrix products, apply_table(): return jnp.einsum(form, table, signal, precision=best_precision)  59.7 us
    all_to_all x2, waiting for transfers between devices, forward(): lax.all_to_all(first_imag, 'seq', split_axis=1, concat_axis=2, tiled=True)  50.5 us
    all_gather x1, waiting for transfers between devices, shards(): piece = lax.all_gather(tokens, 'ch', axis=1, tiled=True)  38.3 us
    all_to_all x2, waiting for transfers between devices, forward(): lax.all_to_all(shaped, 'seq', split_axis=2, concat_axis=1, tiled=True)  36.9 us
    all_to_all x2, waiting for transfers between devices, inverse(): lax.all_to_all(turned_real.astype(jnp.bfloat16), 'seq', split_axis=2, con...  33.1 us
    all_to_all x2, waiting for transfers between devices, inverse(): lax.all_to_all(turned_imag.astype(jnp.bfloat16), 'seq', split_axis=2, con...  27.6 us
    all_to_all x2, starting transfers between devices, forward(): lax.all_to_all(first_imag, 'seq', split_axis=1, concat_axis=2, tiled=True)  22.3 us
  transfers between devices with their start and end apart: 14, of which 14 were waited for; matrix products, arithmetic and copies ran while one was open for 13% of the time, Pallas kernels for 0%

commit v1 on v0

v1 whole, which is shorter than its diff:
```python
import functools
import math

import jax
import jax.numpy as jnp
import numpy as np
from jax import lax
from jax.experimental import pallas as pl
from jax.experimental.pallas import tpu as pltpu
from jax.sharding import PartitionSpec as P

MESH = pl.DeviceIdType.MESH
F32 = jnp.float32
BF16 = jnp.bfloat16
HALO = 16


def tables(blocks, half):
    count = 2 * blocks
    row = np.arange(count)
    q = 2 * (row % blocks) + row // blocks
    k = np.arange(count)
    angle = 2 * np.pi * ((k[:, None] * q[None, :]) % count + q[None, :] / 4) / count
    first = np.concatenate([np.cos(angle), -np.sin(angle)], axis=0)
    last = np.concatenate([np.cos(angle).T, -np.sin(angle).T], axis=1) / (count * half)
    l = np.arange(half)
    twist = 2 * np.pi * (k[:, None] + 0.25) * l[None, :] / (count * half)
    turn = 2 * np.pi * ((l[:, None] * l[None, :]) % half) / half
    c, s = np.cos(turn), np.sin(turn)
    second = np.block([[c, -s], [s, c]])
    third = np.block([[c, s], [-s, c]])
    return (
        jnp.asarray(first, BF16),
        jnp.asarray(second, BF16),
        jnp.asarray(third, BF16),
        jnp.asarray(last, BF16),
        jnp.asarray(np.stack([np.cos(twist), np.sin(twist)]), F32),
    )


def dot(a, b):
    return jnp.dot(a, b, preferred_element_type=F32)


def kernel(
    n, yn,
    tok_ref, wv_ref, wg_ref, taps_ref, skip_ref, filt_ref, gout_ref,
    first_ref, second_ref, third_ref, last_ref, twist_ref,
    out_ref, fgrad_ref,
    tok, wall, taps, skip, filt, gout, first, second, third, last, twist,
    acc, proj, tail, tail_in, value, gate,
    fsend, frecv, vsend, vrecv, csend, crecv, gsend, grecv,
    wide, vwide, mid, spec_v, spec_h, spec_g,
    loc_sem, w_sem, ag_send, ag_recv, tail_sem, f_sem, v_send, v_recv, c_sem, g_sem,
):
    seq = lax.axis_index("seq")
    ch = lax.axis_index("ch")
    rows, dl = tok_ref.shape
    cl = wv_ref.shape[1]
    half = rows // 2
    cpd = cl // n
    count = 2 * n
    right, left = lax.rem(ch + 1, yn), lax.rem(ch + yn - 1, yn)
    far = lax.rem(ch + 2, yn)
    right_id, left_id = (seq, right), (seq, left)

    def local(i, src, dst):
        return pltpu.make_async_copy(src, dst, loc_sem.at[i])

    locals_ = [
        local(0, filt_ref, filt),
        local(1, tok_ref, tok.at[ch]),
        local(2, first_ref, first),
        local(3, second_ref, second),
        local(4, third_ref, third),
        local(5, last_ref, last),
        local(6, twist_ref, twist),
        local(7, taps_ref, taps),
        local(8, skip_ref, skip),
        local(9, gout_ref, gout),
    ]
    for c in locals_[:2]:
        c.start()

    def weight_copies(i, src):
        at = pl.ds(pl.multiple_of(src * dl, dl), dl)
        return [
            pltpu.make_async_copy(wv_ref.at[at], wall.at[at, pl.ds(0, cl)], w_sem.at[2 * i]),
            pltpu.make_async_copy(wg_ref.at[at], wall.at[at, pl.ds(cl, cl)], w_sem.at[2 * i + 1]),
        ]

    weights = [weight_copies(i, s) for i, s in enumerate((ch, left, right, far))]
    for c in weights[0]:
        c.start()
    for c in locals_[2:]:
        c.start()
    for w in weights[1:]:
        for c in w:
            c.start()

    barrier = pltpu.get_barrier_semaphore()

    def greet(k, _):
        pl.semaphore_signal(barrier, inc=1, device_id=(lax.rem(seq + k, n), ch), device_id_type=MESH)
        return 0

    for device in (right_id, left_id):
        pl.semaphore_signal(barrier, inc=1, device_id=device, device_id_type=MESH)
    lax.fori_loop(1, n, greet, 0)

    locals_[0].wait()
    for h in range(2):
        turned = filt[pl.ds(h * half, half), :].T.reshape(n, cpd, half)
        wide[:, pl.ds(h * cpd, cpd), :] = turned
    fsend[...] = wide[...].astype(BF16)

    pl.semaphore_wait(barrier, n - 1 + 2)

    cut = half - HALO
    spans = (pl.ds(cut, rows - cut), pl.ds(0, cut))

    def ag(i, src, dst, device):
        return pltpu.make_async_remote_copy(
            src_ref=src, dst_ref=dst, send_sem=ag_send.at[i], recv_sem=ag_recv.at[i],
            device_id=device, device_id_type=MESH,
        )

    own = [
        [ag(4 * p, tok_ref.at[spans[p]], tok.at[ch, spans[p]], right_id),
         ag(4 * p + 1, tok_ref.at[spans[p]], tok.at[ch, spans[p]], left_id)]
        for p in range(2)
    ]
    low, high = pl.ds(0, dl // 2), pl.ds(dl // 2, dl // 2)

    def forwards(p):
        a, b = tok.at[left, spans[p], low], tok.at[right, spans[p], high]
        return [ag(4 * p + 2, a, a, right_id), ag(4 * p + 3, b, b, left_id)]

    onward = [forwards(p) for p in range(2)]

    def from_neighbour(p, side):
        src = (left, right)[side]
        return ag(4 * p + side, tok.at[src, spans[p]], tok.at[src, spans[p]], (right_id, left_id)[side])

    def from_far(p, side):
        part = tok.at[far, spans[p], (low, high)[side]]
        return ag(4 * p + 2 + side, part, part, (right_id, left_id)[side])

    for c in own[0]:
        c.start()

    def scatter(src, dst, send_sem, recv_sem):
        def one(k, _):
            to = lax.rem(seq + k, n)
            pltpu.make_async_remote_copy(
                src_ref=src.at[to], dst_ref=dst.at[seq], send_sem=send_sem, recv_sem=recv_sem,
                device_id=(to, ch), device_id_type=MESH,
            ).start()
            return 0

        lax.fori_loop(1, n, one, 0)
        dst[seq] = src[seq]

    def await_all(ref, sem):
        part = ref.at[pl.ds(0, n - 1)]
        pltpu.make_async_copy(part, part, sem).wait()

    scatter(fsend, frecv, f_sem.at[0], f_sem.at[1])

    def multiply(p, i, src):
        part = dot(tok[src, spans[p], :], wall[pl.ds(pl.multiple_of(src * dl, dl), dl), :])
        if i == 0:
            acc[spans[p], :] = part
        else:
            acc[spans[p], :] += part

    locals_[1].wait()
    for c in weights[0]:
        c.wait()
    multiply(0, 0, ch)
    multiply(1, 0, ch)

    for side in range(2):
        from_neighbour(0, side).wait_recv()
        onward[0][side].start()
    for c in own[1]:
        c.start()
    for w in weights[1:3]:
        for c in w:
            c.wait()
    multiply(0, 1, left)
    multiply(0, 2, right)

    for c in locals_[2:]:
        c.wait()

    tc, ts = twist[0], twist[1]

    def spectrum(load, spec):
        for pair in range(cpd // 2):
            c0, c1 = 2 * pair, 2 * pair + 1
            x = jnp.concatenate([load(c0), load(c1)], axis=1).astype(BF16)
            a = dot(first[...], x)
            for j, c in enumerate((c0, c1)):
                ar = a[:count, j * half:(j + 1) * half]
                ai = a[count:, j * half:(j + 1) * half]
                mid[pl.ds(c * count, count), pl.ds(0, half)] = (ar * tc + ai * ts).astype(BF16)
                mid[pl.ds(c * count, count), pl.ds(half, half)] = (ai * tc - ar * ts).astype(BF16)
        spec[...] = dot(mid[...], second[...])

    def restore(pr, pi, send):
        mid[:, pl.ds(0, half)] = pr.astype(BF16)
        mid[:, pl.ds(half, half)] = pi.astype(BF16)
        spec_g[...] = dot(mid[...], third[...])
        for pair in range(cpd // 2):
            both = []
            for c in (2 * pair, 2 * pair + 1):
                zr = spec_g[pl.ds(c * count, count), pl.ds(0, half)]
                zi = spec_g[pl.ds(c * count, count), pl.ds(half, half)]
                both.append(jnp.concatenate([zr * tc - zi * ts, zi * tc + zr * ts], axis=0).astype(BF16))
            y = dot(last[...], jnp.concatenate(both, axis=1))
            for j in range(2):
                for h in range(2):
                    vwide[pl.ds(h * cpd + 2 * pair + j, n, stride=2 * cpd), :] = (
                        y[h * n:(h + 1) * n, j * half:(j + 1) * half])
        send[...] = vwide[pl.ds(0, n * 2 * cpd), :].astype(BF16).reshape(n, 2 * cpd, half)

    await_all(frecv, f_sem.at[1])
    vwide[pl.ds(0, n * 2 * cpd), :] = frecv[...].astype(F32).reshape(n * 2 * cpd, half)
    spectrum(
        lambda c: jnp.concatenate(
            [vwide[pl.ds(h * cpd + c, n, stride=2 * cpd), :] for h in range(2)], axis=0),
        spec_h,
    )

    def project(p, h):
        for side in range(2):
            from_far(p, side).wait_recv()
        if p == 0:
            for c in weights[3]:
                c.wait()
        multiply(p, 3, far)
        rounded = acc[spans[p], :].astype(BF16)
        at = spans[p].start + HALO
        proj[pl.ds(at, spans[p].size), :] = rounded.astype(F32)

    def gather_short(h):
        def short(col, tap):
            cols = pl.ds(col, cl)
            return (
                taps[tap:tap + 1, :] * proj[pl.ds(HALO + h * half, half), cols]
                + taps[tap + 1:tap + 2, :] * proj[pl.ds(HALO - 1 + h * half, half), cols]
                + taps[tap + 2:tap + 3, :] * proj[pl.ds(HALO - 2 + h * half, half), cols]
            )

        at = pl.ds(h * half, half)
        v = short(0, 0)
        value[at, :] = v
        g = short(cl, 3)
        gate[at, :] = g
        mixed = gout[at, :].astype(F32) * g
        vsend[h] = jnp.concatenate(
            [v.T.reshape(n, cpd, half), mixed.T.reshape(n, cpd, half)], axis=1
        ).astype(BF16)
        scatter(vsend.at[h], vrecv.at[h], v_send.at[h], v_recv.at[h])

    project(0, 1)
    tail[...] = proj[pl.ds(rows, HALO), :].astype(BF16)
    tail_copy = pltpu.make_async_remote_copy(
        src_ref=tail, dst_ref=tail_in, send_sem=tail_sem.at[0], recv_sem=tail_sem.at[1],
        device_id=(lax.rem(seq + 1, n), ch), device_id_type=MESH,
    )
    tail_copy.start()
    gather_short(1)

    for side in range(2):
        from_neighbour(1, side).wait_recv()
        onward[1][side].start()
    multiply(1, 1, left)
    multiply(1, 2, right)
    tail_copy.wait_recv()
    proj[pl.ds(0, HALO), :] = jnp.where(seq > 0, tail_in[...].astype(F32), 0.0)
    project(1, 0)
    gather_short(0)

    for h in (1, 0):
        await_all(vrecv.at[h], v_recv.at[h])
    vwide[...] = vrecv[...].astype(F32).reshape(2 * n * 2 * cpd, half)

    def branch(offset):
        return lambda c: jnp.concatenate(
            [vwide[pl.ds(h * n * 2 * cpd + offset + c, n, stride=2 * cpd), :] for h in range(2)], axis=0)

    spectrum(branch(0), spec_v)
    spectrum(branch(cpd), spec_g)
    re, im = pl.ds(0, half), pl.ds(half, half)
    gr, gi = spec_g[:, re], spec_g[:, im]
    vr, vi = spec_v[:, re], spec_v[:, im]
    wide_g_r = gr * vr + gi * vi
    wide_g_i = gi * vr - gr * vi
    hr, hi = spec_h[:, re], spec_h[:, im]
    conv_r = vr * hr - vi * hi
    conv_i = vr * hi + vi * hr
    spec_v[:, re] = wide_g_r
    spec_v[:, im] = wide_g_i
    restore(conv_r, conv_i, csend)
    scatter(csend, crecv, c_sem.at[0], c_sem.at[1])
    restore(spec_v[:, re], spec_v[:, im], gsend)
    scatter(gsend, grecv, g_sem.at[0], g_sem.at[1])

    await_all(crecv, c_sem.at[1])
    wide[...] = crecv[...].astype(F32)
    for h in range(2):
        at = pl.ds(h * half, half)
        y = wide[:, pl.ds(h * cpd, cpd), :].reshape(cl, half).T
        out_ref[at, :] = (gate[at, :] * (y + skip[...] * value[at, :])).astype(BF16)
    await_all(grecv, g_sem.at[1])
    wide[...] = grecv[...].astype(F32)
    for h in range(2):
        at = pl.ds(h * half, half)
        fgrad_ref[at, :] = wide[:, pl.ds(h * cpd, cpd), :].reshape(cl, half).T

    for c in own[0] + own[1] + onward[0] + onward[1] + [tail_copy]:
        c.wait_send()
    await_all(fsend, f_sem.at[0])
    for h in range(2):
        await_all(vsend.at[h], v_send.at[h])
    await_all(csend, c_sem.at[0])
    await_all(gsend, g_sem.at[0])


def shards(n, yn, tokens, w_value, w_gate, short_value, short_gate, skip_bias, long_filter, grad_out):
    rows, dl = tokens.shape
    d, cl = w_value.shape
    half = rows // 2
    cpd = cl // n
    count = 2 * n
    taps = jnp.concatenate([short_value, short_gate], axis=0)
    consts = tables(n, half)
    block = (n, 2 * cpd, half)
    anywhere = pl.BlockSpec(memory_space=pl.ANY)
    vmem = pl.BlockSpec(memory_space=pltpu.VMEM)
    dma = pltpu.SemaphoreType.DMA
    scratch = [
        pltpu.VMEM((yn, rows, dl), BF16),
        pltpu.VMEM((d, 2 * cl), BF16),
        pltpu.VMEM((6, cl), F32),
        pltpu.VMEM((1, cl), F32),
        pltpu.VMEM((rows, cl), F32),
        pltpu.VMEM((rows, cl), BF16),
        *[pltpu.VMEM(c.shape, c.dtype) for c in consts],
        pltpu.VMEM((rows, 2 * cl), F32),
        pltpu.VMEM((HALO + rows, 2 * cl), F32),
        pltpu.VMEM((HALO, 2 * cl), BF16),
        pltpu.VMEM((HALO, 2 * cl), BF16),
        pltpu.VMEM((rows, cl), F32),
        pltpu.VMEM((rows, cl), F32),
        pltpu.VMEM(block, BF16),
        pltpu.VMEM(block, BF16),
        pltpu.VMEM((2, *block), BF16),
        pltpu.VMEM((2, *block), BF16),
        pltpu.VMEM(block, BF16),
        pltpu.VMEM(block, BF16),
        pltpu.VMEM(block, BF16),
        pltpu.VMEM(block, BF16),
        pltpu.VMEM(block, F32),
        pltpu.VMEM((2 * n * 2 * cpd, half), F32),
        pltpu.VMEM((cpd * count, 2 * half), BF16),
        pltpu.VMEM((cpd * count, 2 * half), F32),
        pltpu.VMEM((cpd * count, 2 * half), F32),
        pltpu.VMEM((cpd * count, 2 * half), F32),
        dma((10,)),
        dma((2 * yn,)),
        dma((8,)),
        dma((8,)),
        dma((2,)),
        dma((2,)),
        dma((2,)),
        dma((2,)),
        dma((2,)),
        dma((2,)),
    ]
    return pl.pallas_call(
        functools.partial(kernel, n, yn),
        out_shape=(
            jax.ShapeDtypeStruct((rows, cl), BF16),
            jax.ShapeDtypeStruct((rows, cl), F32),
        ),
        in_specs=[anywhere] * 12,
        out_specs=(vmem, vmem),
        scratch_shapes=scratch,
        compiler_params=pltpu.CompilerParams(
            collective_id=0, has_side_effects=True, vmem_limit_bytes=56 * 1024 * 1024
        ),
    )(tokens, w_value, w_gate, taps, skip_bias[None], long_filter, grad_out, *consts)


def solution(mesh):
    return jax.shard_map(
        functools.partial(shards, mesh.shape["seq"], mesh.shape["ch"]),
        mesh=mesh,
        in_specs=(
            P("seq", "ch"),
            P(None, "ch"),
            P(None, "ch"),
            P(None, "ch"),
            P(None, "ch"),
            P("ch"),
            P("seq", "ch"),
            P("seq", "ch"),
        ),
        out_specs=(P("seq", "ch"), P("seq", "ch")),
        check_vma=False,
    )
```

time: 513 us -> 68.8 us (0.13); the launches traced: 503 us -> 68.6 us
  waiting for transfers between devices: 273 us -> 0 us
  starting transfers between devices: 92.6 us -> 0 us
  matrix products: 65.2 us -> 0 us
  Pallas kernels: 0 us -> 63.1 us
  local copies, waits for them, and re-layouts: 47.6 us -> 3.54 us
  between operations: 15.1 us -> 0.64 us
  other arithmetic: 9.63 us -> 1.33 us
    all_to_all x12 -> x0, waiting for transfers between devices: 234 us -> none  [the longest x2 63.5 us: forward(): lax.all_to_all(first_real, 'seq', split_axis=1, concat_axis=2, tiled=True)]
    all_to_all x12 -> x0, starting transfers between devices: 89 us -> none  [the longest x2 22.3 us: forward(): lax.all_to_all(first_imag, 'seq', split_axis=1, concat_axis=2, tiled=True)]
    dot_general x26 -> x0, matrix products: 65.2 us -> none  [the longest x24 59.7 us: apply_table(): return jnp.einsum(form, table, signal, precision=best_precision)]
    pallas_call x0 -> x1, Pallas kernels: none -> 63.1 us  [shards(): pl.pallas_call(functools.partial(kernel, n, yn), out_shape=(jax.ShapeDtyp...]
    all_gather x1 -> x0, waiting for transfers between devices: 38.3 us -> none  [shards(): piece = lax.all_gather(tokens, 'ch', axis=1, tiled=True)]
    all_to_all x8 -> x0, local copies, waits for them, and re-layouts: 11.8 us -> none  [the longest x2 4.98 us: forward(): lax.all_to_all(first_real, 'seq', split_axis=1, concat_axis=2, tiled=True)]
    convert_element_type x8 -> x0, local copies, waits for them, and re-layouts: 7.38 us -> none  [the longest x2 2.35 us: inverse(): turned_real.astype(jnp.bfloat16)]
    sub x2 -> x0, local copies, waits for them, and re-layouts: 6 us -> none  [forward(): turned_imag = imag_part * twist_cos - real_part * twist_sin]
  transfers between devices with their start and end apart: 14 -> 0, of which waited for: 14 -> 0; matrix products, arithmetic and copies ran while one was open for 13% -> 0% of each run, Pallas kernels for 0% -> 0%
where the time goes in v1:
time: 68.8 us; the launch traced here: 68.6 us
  Pallas kernels  63.1 us (92%)
  local copies, waits for them, and re-layouts  3.54 us (5%)
  other arithmetic  1.33 us (2%)
    pallas_call x1, Pallas kernels, shards(): pl.pallas_call(functools.partial(kernel, n, yn), out_shape=(jax.ShapeDtyp...  63.1 us
    unnamed x2, local copies, waits for them, and re-layouts  3.54 us

profile of v1, /device:TPU:1, one launch (start us, length us, event | category | flops | bytes accessed | tf_op | source)
XLA Modules:
  0.0 68.6 jit_solution(14440137665486406489)
XLA Ops:
  0.6 1.3 %pad_maximum_fusion.taps_ref = f32[6,512]{1,0:T(8,128)} fusion(f32[3,512]{1,0:T(4,128)} %param.17, f32[3,512]{1,0:T(4,128)} %param.16), kind=kLoop, calls=%fused_computation | loop fusion | flops 3072 | bytes 24576 | tf_op jit(solution)/shard_map/concatenate | solution.py:338
  2.0 63.1 %shard_map.140 = (bf16[256,512]{1,0:T(8,128)(2,1)}, f32[256,512]{1,0:T(8,128)}) custom-call(bf16[256,1024]{1,0:T(8,128)(2,1)} %tok_ref.1, bf16[4096,512]{1,0:T(8,128)(2,1)} %wv_ref.1, bf16[4096,512]{1,0:T(8,128)(2,1)} %wg_ref.1, f32[6,512]{1,0:T(8,128)} %pad_maximum_fusion.taps_ref, f32[1,512]{1,0:T(1,128)} %bitcast.1, f32[256,512]{1,0:T(8,128)} %filt_ref.1, ...), custom_call_target="tpu_custom_call" | custom-call | tf_op jit(solution)/shard_map/pallas_call | solution.py:383
  65.1 1.7 %copy.17 = bf16[256,512]{1,0:T(8,128)(2,1)} copy(bf16[256,512]{1,0:T(8,128)(2,1)} %get-tuple-element.4) | data formatting | bytes 524288
  66.8 1.9 %copy.18 = f32[256,512]{1,0:T(8,128)} copy(f32[256,512]{1,0:T(8,128)} %get-tuple-element.5) | data formatting | bytes 1048576

commit v2 on v1

v2 whole, which is shorter than its diff:
```python
import functools
import math

import jax
import jax.numpy as jnp
import numpy as np
from jax import lax
from jax.experimental import pallas as pl
from jax.experimental.pallas import tpu as pltpu
from jax.sharding import PartitionSpec as P

MESH = pl.DeviceIdType.MESH
F32 = jnp.float32
BF16 = jnp.bfloat16
HALO = 16


def tables(blocks, half):
    count = 2 * blocks
    row = np.arange(count)
    q = 2 * (row % blocks) + row // blocks
    k = np.arange(count)
    angle = 2 * np.pi * ((k[:, None] * q[None, :]) % count + q[None, :] / 4) / count
    first = np.concatenate([np.cos(angle), -np.sin(angle)], axis=0)
    last = np.concatenate([np.cos(angle).T, -np.sin(angle).T], axis=1) / (count * half)
    l = np.arange(half)
    twist = 2 * np.pi * (k[:, None] + 0.25) * l[None, :] / (count * half)
    turn = 2 * np.pi * ((l[:, None] * l[None, :]) % half) / half
    c, s = np.cos(turn), np.sin(turn)
    second = np.block([[c, -s], [s, c]])
    third = np.block([[c, s], [-s, c]])
    return (
        jnp.asarray(first, BF16),
        jnp.asarray(second, BF16),
        jnp.asarray(third, BF16),
        jnp.asarray(last, BF16),
        jnp.asarray(np.stack([np.cos(twist), np.sin(twist)]), F32),
    )


def dot(a, b):
    return jnp.dot(a, b, preferred_element_type=F32)


def transform_kernel(
    n, yn,
    tok_ref, wv_ref, wg_ref, taps_v_ref, taps_g_ref, skip_ref, filt_ref, gout_ref,
    first_ref, second_ref, third_ref, last_ref, twist_ref,
    crecv, grecv, gate_ref, base_ref,
    tok, wall, taps_v, taps_g, skip, filt, gout, first, second, third, last, twist,
    acc, proj, tail, tail_in, gate, base,
    fsend, frecv, asend, arecv, vsend, vrecv, msend, mrecv, csend, gsend,
    wide, fwide, awide, vwide, mwide, mid, spec_v, spec_h, spec_g,
    loc_sem, w_sem, ag_send, ag_recv, tail_sem, own_sem,
    f_sem, a_sem, v_sem, m_sem, c_sem, g_sem, met,
):
    seq = lax.axis_index("seq")
    ch = lax.axis_index("ch")
    rows, dl = tok_ref.shape
    cl = wv_ref.shape[1]
    half = rows // 2
    cpd = cl // n
    count = 2 * n
    group = 8 if n >= 32 else 1
    zs = n // group
    right, left = lax.rem(ch + 1, yn), lax.rem(ch + yn - 1, yn)
    far = lax.rem(ch + 2, yn)
    right_id, left_id = (seq, right), (seq, left)
    z, mate = seq // group, lax.rem(seq, group)

    def along_z(k):
        return (lax.rem(z + k + zs, zs) * group + mate, ch)

    def in_group(k):
        return (z * group + lax.rem(mate + k, group), ch)

    def local(i, src, dst):
        return pltpu.make_async_copy(src, dst, loc_sem.at[i])

    locals_ = [
        local(0, filt_ref, filt),
        local(1, tok_ref, tok.at[ch]),
        local(2, first_ref, first),
        local(3, second_ref, second),
        local(4, third_ref, third),
        local(5, last_ref, last),
        local(6, twist_ref, twist),
        local(7, taps_v_ref, taps_v),
        local(8, taps_g_ref, taps_g),
        local(9, skip_ref, skip),
        local(10, gout_ref, gout),
    ]

    def weight_copies(i, src):
        at = pl.ds(pl.multiple_of(src * dl, dl), dl)
        return [
            pltpu.make_async_copy(wv_ref.at[at], wall.at[at, pl.ds(0, cl)], w_sem.at[2 * i]),
            pltpu.make_async_copy(wg_ref.at[at], wall.at[at, pl.ds(cl, cl)], w_sem.at[2 * i + 1]),
        ]

    weights = [weight_copies(i, s) for i, s in enumerate((ch, left, right, far))]

    barrier = pltpu.get_barrier_semaphore()
    near = [right_id, left_id, along_z(1), along_z(-1)] + [in_group(k) for k in range(1, group)]
    for device in near:
        pl.semaphore_signal(barrier, inc=1, device_id=device, device_id_type=MESH)
    for c in locals_[:2] + weights[0] + locals_[2:]:
        c.start()
    for w in weights[1:]:
        for c in w:
            c.start()
    pl.semaphore_wait(barrier, len(near))

    cut = half - HALO
    spans = (pl.ds(cut, rows - cut), pl.ds(0, cut))

    def ag(i, src, dst, device):
        return pltpu.make_async_remote_copy(
            src_ref=src, dst_ref=dst, send_sem=ag_send.at[i], recv_sem=ag_recv.at[i],
            device_id=device, device_id_type=MESH,
        )

    own = [
        [ag(4 * p, tok_ref.at[spans[p]], tok.at[ch, spans[p]], right_id),
         ag(4 * p + 1, tok_ref.at[spans[p]], tok.at[ch, spans[p]], left_id)]
        for p in range(2)
    ]
    low, high = pl.ds(0, dl // 2), pl.ds(dl // 2, dl // 2)

    def forwards(p):
        a, b = tok.at[left, spans[p], low], tok.at[right, spans[p], high]
        return [ag(4 * p + 2, a, a, right_id), ag(4 * p + 3, b, b, left_id)]

    onward = [forwards(p) for p in range(2)]

    def from_neighbour(p, side):
        src = (left, right)[side]
        return ag(4 * p + side, tok.at[src, spans[p]], tok.at[src, spans[p]], (right_id, left_id)[side])

    def from_far(p, side):
        part = tok.at[far, spans[p], (low, high)[side]]
        return ag(4 * p + 2 + side, part, part, (right_id, left_id)[side])

    for c in own[0] + own[1]:
        c.start()

    def multiply(p, i, src, cols):
        part = dot(tok[src, spans[p], :], wall[pl.ds(pl.multiple_of(src * dl, dl), dl), cols])
        if i == 0:
            acc[spans[p], cols] = part
        else:
            acc[spans[p], cols] += part

    both = pl.ds(0, 2 * cl)

    rounds = [[along_z(1), along_z(-1)]]
    if zs > 4:
        rounds.append([along_z(2), along_z(-2)])
    if group > 1:
        rounds.append([in_group(k) for k in range(1, group)])

    def meet(r):
        for device in rounds[r]:
            pl.semaphore_signal(met.at[r], inc=1, device_id=device, device_id_type=MESH)

    def met_all(r):
        pl.semaphore_wait(met.at[r], len(rounds[r]))

    meet(0)
    locals_[0].wait()
    for h in range(2):
        turned = filt[pl.ds(h * half, half), :].T.reshape(n, cpd, half)
        wide[:, pl.ds(h * cpd, cpd), :] = turned
    fsend[...] = wide[...].astype(BF16)
    met_all(0)
    for r in range(1, len(rounds)):
        meet(r)
        if r == 1:
            locals_[1].wait()
            for c in weights[0]:
                c.wait()
            multiply(0, 0, ch, both)
        met_all(r)
    if len(rounds) < 2:
        locals_[1].wait()
        for c in weights[0]:
            c.wait()
        multiply(0, 0, ch, both)

    def scatter(src, dst, sem):
        def one(k, _):
            to = lax.rem(seq + k, n)
            pltpu.make_async_remote_copy(
                src_ref=src.at[to], dst_ref=dst.at[seq], send_sem=sem.at[0], recv_sem=sem.at[1],
                device_id=(to, ch), device_id_type=MESH,
            ).start()
            return 0

        lax.fori_loop(1, n, one, 0)

    def await_all(ref, sem):
        part = ref.at[pl.ds(0, n - 1)]
        pltpu.make_async_copy(part, part, sem).wait()

    scatter(fsend, frecv, f_sem)
    frecv[seq] = fsend[seq]
    multiply(1, 0, ch, both)

    for side in range(2):
        from_neighbour(0, side).wait_recv()
        onward[0][side].start()
    for w in weights[1:3]:
        for c in w:
            c.wait()
    multiply(0, 1, left, both)
    multiply(0, 2, right, both)
    for c in locals_[2:]:
        c.wait()

    tc, ts = twist[0], twist[1]

    def spectrum(load, spec):
        for pair in range(cpd // 2):
            c0, c1 = 2 * pair, 2 * pair + 1
            x = jnp.concatenate([load(c0), load(c1)], axis=1).astype(BF16)
            a = dot(first[...], x)
            for j, c in enumerate((c0, c1)):
                ar = a[:count, j * half:(j + 1) * half]
                ai = a[count:, j * half:(j + 1) * half]
                mid[pl.ds(c * count, count), pl.ds(0, half)] = (ar * tc + ai * ts).astype(BF16)
                mid[pl.ds(c * count, count), pl.ds(half, half)] = (ai * tc - ar * ts).astype(BF16)
        spec[...] = dot(mid[...], second[...])

    def restore(pr, pi, send):
        mid[:, pl.ds(0, half)] = pr.astype(BF16)
        mid[:, pl.ds(half, half)] = pi.astype(BF16)
        spec_g[...] = dot(mid[...], third[...])
        for pair in range(cpd // 2):
            two = []
            for c in (2 * pair, 2 * pair + 1):
                zr = spec_g[pl.ds(c * count, count), pl.ds(0, half)]
                zi = spec_g[pl.ds(c * count, count), pl.ds(half, half)]
                two.append(jnp.concatenate([zr * tc - zi * ts, zi * tc + zr * ts], axis=0).astype(BF16))
            y = dot(last[...], jnp.concatenate(two, axis=1))
            for j in range(2):
                for h in range(2):
                    fwide[pl.ds(h * cpd + 2 * pair + j, n, stride=2 * cpd), :] = (
                        y[h * n:(h + 1) * n, j * half:(j + 1) * half])
        send[...] = fwide[...].astype(BF16).reshape(n, 2 * cpd, half)

    def rows_of(low_ref, low_at, low_stride, high_ref, high_at, high_stride):
        return lambda c: jnp.concatenate(
            [low_ref[pl.ds(low_at + c, n, stride=low_stride), :],
             high_ref[pl.ds(high_at + c, n, stride=high_stride), :]], axis=0)

    await_all(frecv, f_sem.at[1])
    fwide[...] = frecv[...].astype(F32).reshape(n * 2 * cpd, half)
    spectrum(rows_of(fwide, 0, 2 * cpd, fwide, cpd, 2 * cpd), spec_h)

    def short(h, taps, col):
        cols = pl.ds(col, cl)
        return (
            taps[0:1, :] * proj[pl.ds(HALO + h * half, half), cols]
            + taps[1:2, :] * proj[pl.ds(HALO - 1 + h * half, half), cols]
            + taps[2:3, :] * proj[pl.ds(HALO - 2 + h * half, half), cols]
        )

    def finish(p, cols):
        proj[pl.ds(spans[p].start + HALO, spans[p].size), cols] = acc[spans[p], cols].astype(BF16).astype(F32)

    def gated(h, v):
        at = pl.ds(h * half, half)
        g = short(h, taps_g, cl)
        gate[at, :] = g
        base[at, :] = g * skip[...] * v
        return gout[at, :].astype(F32) * g

    for side in range(2):
        from_neighbour(1, side).wait_recv()
        onward[1][side].start()

    for side in range(2):
        from_far(0, side).wait_recv()
    for c in weights[3]:
        c.wait()
    multiply(0, 3, far, both)
    finish(0, both)
    tail[...] = proj[pl.ds(rows, HALO), :].astype(BF16)
    tail_copy = pltpu.make_async_remote_copy(
        src_ref=tail, dst_ref=tail_in, send_sem=tail_sem.at[0], recv_sem=tail_sem.at[1],
        device_id=(lax.rem(seq + 1, n), ch), device_id_type=MESH,
    )
    tail_copy.start()
    v = short(1, taps_v, 0)
    mixed = gated(1, v)
    asend[...] = jnp.concatenate(
        [v.T.reshape(n, cpd, half), mixed.T.reshape(n, cpd, half)], axis=1).astype(BF16)
    scatter(asend, arecv, a_sem)
    arecv[seq] = asend[seq]

    multiply(1, 1, left, both)
    multiply(1, 2, right, both)
    tail_copy.wait_recv()
    proj[pl.ds(0, HALO), :] = jnp.where(seq > 0, tail_in[...].astype(F32), 0.0)
    value_cols, gate_cols = pl.ds(0, cl), pl.ds(cl, cl)
    for side in range(2):
        from_far(1, side).wait_recv()
    multiply(1, 3, far, value_cols)
    finish(1, value_cols)
    v = short(0, taps_v, 0)
    vsend[...] = v.T.reshape(n, cpd, half).astype(BF16)
    scatter(vsend, vrecv, v_sem)
    vrecv[seq] = vsend[seq]
    multiply(1, 3, far, gate_cols)
    finish(1, gate_cols)
    mixed = gated(0, v)
    msend[...] = mixed.T.reshape(n, cpd, half).astype(BF16)
    scatter(msend, mrecv, m_sem)
    mrecv[seq] = msend[seq]
    results = [local(0, gate, gate_ref), local(1, base, base_ref)]
    for c in results:
        c.start()

    await_all(arecv, a_sem.at[1])
    awide[...] = arecv[...].astype(F32).reshape(n * 2 * cpd, half)
    await_all(vrecv, v_sem.at[1])
    vwide[...] = vrecv[...].astype(F32).reshape(n * cpd, half)
    spectrum(rows_of(vwide, 0, cpd, awide, 0, 2 * cpd), spec_v)
    re, im = pl.ds(0, half), pl.ds(half, half)
    vr, vi = spec_v[:, re], spec_v[:, im]
    hr, hi = spec_h[:, re], spec_h[:, im]
    restore(vr * hr - vi * hi, vr * hi + vi * hr, csend)
    scatter(csend, crecv, c_sem)
    stays = [pltpu.make_async_copy(csend.at[seq], crecv.at[seq], own_sem.at[0])]
    stays[0].start()

    await_all(mrecv, m_sem.at[1])
    mwide[...] = mrecv[...].astype(F32).reshape(n * cpd, half)
    spectrum(rows_of(mwide, 0, cpd, awide, cpd, 2 * cpd), spec_g)
    gr, gi = spec_g[:, re], spec_g[:, im]
    vr, vi = spec_v[:, re], spec_v[:, im]
    restore(gr * vr + gi * vi, gi * vr - gr * vi, gsend)
    scatter(gsend, grecv, g_sem)
    stays.append(pltpu.make_async_copy(gsend.at[seq], grecv.at[seq], own_sem.at[1]))
    stays[1].start()

    for c in own[0] + own[1] + onward[0] + onward[1] + [tail_copy]:
        c.wait_send()
    for c in results + stays:
        c.wait()
    for ref, sem in ((fsend, f_sem), (asend, a_sem), (vsend, v_sem), (msend, m_sem)):
        await_all(ref, sem.at[0])
    await_all(crecv, c_sem.at[1])
    await_all(csend, c_sem.at[0])
    await_all(grecv, g_sem.at[1])
    await_all(gsend, g_sem.at[0])


def closing_kernel(conv_ref, grad_ref, gate_ref, base_ref, out_ref, fgrad_ref):
    cpd = conv_ref.shape[1] // 2
    half = conv_ref.shape[2]
    columns = out_ref.shape[1]

    def turned(ref, h):
        return ref[...].astype(F32)[:, h * cpd:(h + 1) * cpd, :].reshape(columns, half).T

    for h in range(2):
        at = pl.ds(h * half, half)
        out_ref[at, :] = (gate_ref[at, :] * turned(conv_ref, h) + base_ref[at, :]).astype(BF16)
        fgrad_ref[at, :] = turned(grad_ref, h)


def shards(n, yn, tokens, w_value, w_gate, short_value, short_gate, skip_bias, long_filter, grad_out):
    rows, dl = tokens.shape
    d, cl = w_value.shape
    half = rows // 2
    cpd = cl // n
    count = 2 * n
    consts = tables(n, half)
    block = (n, 2 * cpd, half)
    small = (n, cpd, half)
    anywhere = pl.BlockSpec(memory_space=pl.ANY)
    dma = pltpu.SemaphoreType.DMA
    scratch = [
        pltpu.VMEM((yn, rows, dl), BF16),
        pltpu.VMEM((d, 2 * cl), BF16),
        pltpu.VMEM((3, cl), F32),
        pltpu.VMEM((3, cl), F32),
        pltpu.VMEM((1, cl), F32),
        pltpu.VMEM((rows, cl), F32),
        pltpu.VMEM((rows, cl), BF16),
        *[pltpu.VMEM(c.shape, c.dtype) for c in consts],
        pltpu.VMEM((rows, 2 * cl), F32),
        pltpu.VMEM((HALO + rows, 2 * cl), F32),
        pltpu.VMEM((HALO, 2 * cl), BF16),
        pltpu.VMEM((HALO, 2 * cl), BF16),
        pltpu.VMEM((rows, cl), F32),
        pltpu.VMEM((rows, cl), F32),
        pltpu.VMEM(block, BF16),
        pltpu.VMEM(block, BF16),
        pltpu.VMEM(block, BF16),
        pltpu.VMEM(block, BF16),
        pltpu.VMEM(small, BF16),
        pltpu.VMEM(small, BF16),
        pltpu.VMEM(small, BF16),
        pltpu.VMEM(small, BF16),
        pltpu.VMEM(block, BF16),
        pltpu.VMEM(block, BF16),
        pltpu.VMEM(block, F32),
        pltpu.VMEM((n * 2 * cpd, half), F32),
        pltpu.VMEM((n * 2 * cpd, half), F32),
        pltpu.VMEM((n * cpd, half), F32),
        pltpu.VMEM((n * cpd, half), F32),
        pltpu.VMEM((cpd * count, 2 * half), BF16),
        pltpu.VMEM((cpd * count, 2 * half), F32),
        pltpu.VMEM((cpd * count, 2 * half), F32),
        pltpu.VMEM((cpd * count, 2 * half), F32),
        dma((11,)),
        dma((2 * yn,)),
        dma((8,)),
        dma((8,)),
        dma((2,)),
        dma((2,)),
        dma((2,)),
        dma((2,)),
        dma((2,)),
        dma((2,)),
        dma((2,)),
        dma((2,)),
        pltpu.SemaphoreType.REGULAR((3,)),
    ]
    conv, grad, gate, base = pl.pallas_call(
        functools.partial(transform_kernel, n, yn),
        out_shape=(
            jax.ShapeDtypeStruct(block, BF16),
            jax.ShapeDtypeStruct(block, BF16),
            jax.ShapeDtypeStruct((rows, cl), F32),
            jax.ShapeDtypeStruct((rows, cl), F32),
        ),
        in_specs=[anywhere] * 13,
        out_specs=[anywhere] * 4,
        scratch_shapes=scratch,
        compiler_params=pltpu.CompilerParams(
            collective_id=0, has_side_effects=True, vmem_limit_bytes=56 * 1024 * 1024
        ),
    )(tokens, w_value, w_gate, short_value, short_gate, skip_bias[None], long_filter, grad_out, *consts)
    steps = 2
    blocks = pl.BlockSpec((n // steps, 2 * cpd, half), lambda i: (i, 0, 0))
    columns = pl.BlockSpec((rows, cl // steps), lambda i: (0, i))
    return pl.pallas_call(
        closing_kernel,
        grid=(steps,),
        out_shape=(
            jax.ShapeDtypeStruct((rows, cl), BF16),
            jax.ShapeDtypeStruct((rows, cl), F32),
        ),
        in_specs=[blocks, blocks, columns, columns],
        out_specs=(columns, columns),
    )(conv, grad, gate, base)


def solution(mesh):
    return jax.shard_map(
        functools.partial(shards, mesh.shape["seq"], mesh.shape["ch"]),
        mesh=mesh,
        in_specs=(
            P("seq", "ch"),
            P(None, "ch"),
            P(None, "ch"),
            P(None, "ch"),
            P(None, "ch"),
            P("ch"),
            P("seq", "ch"),
            P("seq", "ch"),
        ),
        out_specs=(P("seq", "ch"), P("seq", "ch")),
        check_vma=False,
    )
```

time: 68.8 us -> 60.7 us (0.88)
  local copies, waits for them, and re-layouts: 3.54 us -> 0 us
  Pallas kernels: 63.1 us -> 59.9 us
  other arithmetic: 1.33 us -> 0 us
    unnamed x2 -> x0, local copies, waits for them, and re-layouts: 3.54 us -> none
    pallas_call x1 -> x2, Pallas kernels: 63.1 us -> 59.9 us  [the longest x1 57.6 us: shards(): pl.pallas_call(functools.partial(transform_kernel, n, yn), out_shape=(jax...]
    concatenate x1 -> x0, other arithmetic: 1.33 us -> none  [shards(): taps = jnp.concatenate([short_value, short_gate], axis=0)]
where the time goes in v2:
time: 60.7 us; the launch traced here: 60.6 us
  Pallas kernels  59.9 us (99%)
  between operations  0.64 us (1%)
    pallas_call x1, Pallas kernels, shards(): pl.pallas_call(functools.partial(transform_kernel, n, yn), out_shape=(jax...  57.6 us
    pallas_call x1, Pallas kernels, shards(): pl.pallas_call(closing_kernel, grid=(steps,), out_shape=(jax.ShapeDtypeSt...  2.31 us

profile of v2, /device:TPU:1, one launch (start us, length us, event | category | flops | bytes accessed | tf_op | source)
XLA Modules:
  0.0 60.6 jit_solution(6448822740171160253)
XLA Ops:
  0.6 57.6 %shard_map.140 = (bf16[64,16,128]{2,1,0:T(8,128)(2,1)}, bf16[64,16,128]{2,1,0:T(8,128)(2,1)}, f32[256,512]{1,0:T(8,128)}, f32[256,512]{1,0:T(8,128)}) custom-call(bf16[256,1024]{1,0:T(8,128)(2,1)} %tok_ref.1, bf16[4096,512]{1,0:T(8,128)(2,1)} %wv_ref.1, bf16[4096,512]{1,0:T(8,128)(2,1)} %wg_ref.1, f32[3,512]{1,0:T(4,128)} %taps_v_ref.1, ...), custom_call_target="tpu_custom_call" | custom-call | tf_op jit(solution)/shard_map/pallas_call | solution.py:432
  58.3 2.3 %shard_map.141 = (bf16[256,512]{1,0:T(8,128)(2,1)}, f32[256,512]{1,0:T(8,128)}) custom-call(bf16[64,16,128]{2,1,0:T(8,128)(2,1)} %get-tuple-element.6.conv_ref, bf16[64,16,128]{2,1,0:T(8,128)(2,1)} %get-tuple-element.7.grad_ref, f32[256,512]{1,0:T(8,128)} %get-tuple-element.8.gate_ref, f32[256,512]{1,0:T(8,128)} %get-tuple-element.9.base_ref), custom_call_target="tpu_custom_call" | custom-call | tf_op jit(solution)/shard_map/pallas_call | solution.py:450

commit v3 on v2

--- a/solution.py
+++ b/solution.py
@@ -49,10 +49,10 @@
     crecv, grecv, gate_ref, base_ref,
     tok, wall, taps_v, taps_g, skip, filt, gout, first, second, third, last, twist,
     acc, proj, tail, tail_in, gate, base,
-    fsend, frecv, asend, arecv, vsend, vrecv, msend, mrecv, csend, gsend,
-    wide, fwide, awide, vwide, mwide, mid, spec_v, spec_h, spec_g,
+    fsend, frecv, vsend, vrecv, msend, mrecv, csend, gsend,
+    wide, fwide, vwide, mid, spec_v, spec_h, spec_g,
     loc_sem, w_sem, ag_send, ag_recv, tail_sem, own_sem,
-    f_sem, a_sem, v_sem, m_sem, c_sem, g_sem, met,
+    f_sem, v_sem, m_sem, c_sem, g_sem, met,
 ):
     seq = lax.axis_index("seq")
     ch = lax.axis_index("ch")
@@ -104,15 +104,16 @@
     near = [right_id, left_id, along_z(1), along_z(-1)] + [in_group(k) for k in range(1, group)]
     for device in near:
         pl.semaphore_signal(barrier, inc=1, device_id=device, device_id_type=MESH)
-    for c in locals_[:2] + weights[0] + locals_[2:]:
+    for c in locals_:
         c.start()
-    for w in weights[1:]:
+    for w in weights:
         for c in w:
             c.start()
     pl.semaphore_wait(barrier, len(near))
 
     cut = half - HALO
     spans = (pl.ds(cut, rows - cut), pl.ds(0, cut))
+    pieces = spans
 
     def ag(i, src, dst, device):
         return pltpu.make_async_remote_copy(
@@ -121,24 +122,25 @@
         )
 
     own = [
-        [ag(4 * p, tok_ref.at[spans[p]], tok.at[ch, spans[p]], right_id),
-         ag(4 * p + 1, tok_ref.at[spans[p]], tok.at[ch, spans[p]], left_id)]
-        for p in range(2)
+        [ag(4 * p, tok_ref.at[at], tok.at[ch, at], right_id),
+         ag(4 * p + 1, tok_ref.at[at], tok.at[ch, at], left_id)]
+        for p, at in enumerate(pieces)
     ]
     low, high = pl.ds(0, dl // 2), pl.ds(dl // 2, dl // 2)
 
     def forwards(p):
-        a, b = tok.at[left, spans[p], low], tok.at[right, spans[p], high]
+        a, b = tok.at[left, pieces[p], low], tok.at[right, pieces[p], high]
         return [ag(4 * p + 2, a, a, right_id), ag(4 * p + 3, b, b, left_id)]
 
-    onward = [forwards(p) for p in range(2)]
+    onward = [forwards(p) for p in range(len(pieces))]
 
     def from_neighbour(p, side):
         src = (left, right)[side]
-        return ag(4 * p + side, tok.at[src, spans[p]], tok.at[src, spans[p]], (right_id, left_id)[side])
+        part = tok.at[src, pieces[p]]
+        return ag(4 * p + side, part, part, (right_id, left_id)[side])
 
     def from_far(p, side):
-        part = tok.at[far, spans[p], (low, high)[side]]
+        part = tok.at[far, pieces[p], (low, high)[side]]
         return ag(4 * p + 2 + side, part, part, (right_id, left_id)[side])
 
     for c in own[0] + own[1]:
@@ -189,14 +191,18 @@
 
     def scatter(src, dst, sem):
         def one(k, _):
-            to = lax.rem(seq + k, n)
+            j, r = lax.rem(k, zs), group - 1 - k // zs
+            odd = lax.rem(j, 2)
+            dz = zs // 2 + (j // 2) * (1 - odd) - ((j + 1) // 2) * odd
+            x = lax.rem(mate // 2 + r // 2, max(group // 2, 1))
+            to = lax.rem(z + dz, zs) * group + x * 2 + lax.rem(mate + r, min(group, 2))
             pltpu.make_async_remote_copy(
                 src_ref=src.at[to], dst_ref=dst.at[seq], send_sem=sem.at[0], recv_sem=sem.at[1],
                 device_id=(to, ch), device_id_type=MESH,
             ).start()
             return 0
 
-        lax.fori_loop(1, n, one, 0)
+        lax.fori_loop(0, n - 1, one, 0)
 
     def await_all(ref, sem):
         part = ref.at[pl.ds(0, n - 1)]
@@ -206,9 +212,12 @@
     frecv[seq] = fsend[seq]
     multiply(1, 0, ch, both)
 
-    for side in range(2):
-        from_neighbour(0, side).wait_recv()
-        onward[0][side].start()
+    def pass_on(p):
+        for side in range(2):
+            from_neighbour(p, side).wait_recv()
+            onward[p][side].start()
+
+    pass_on(0)
     for w in weights[1:3]:
         for c in w:
             c.wait()
@@ -253,9 +262,6 @@
             [low_ref[pl.ds(low_at + c, n, stride=low_stride), :],
              high_ref[pl.ds(high_at + c, n, stride=high_stride), :]], axis=0)
 
-    await_all(frecv, f_sem.at[1])
-    fwide[...] = frecv[...].astype(F32).reshape(n * 2 * cpd, half)
-    spectrum(rows_of(fwide, 0, 2 * cpd, fwide, cpd, 2 * cpd), spec_h)
 
     def short(h, taps, col):
         cols = pl.ds(col, cl)
@@ -275,9 +281,8 @@
         base[at, :] = g * skip[...] * v
         return gout[at, :].astype(F32) * g
 
-    for side in range(2):
-        from_neighbour(1, side).wait_recv()
-        onward[1][side].start()
+    for p in range(1, len(pieces)):
+        pass_on(p)
 
     for side in range(2):
         from_far(0, side).wait_recv()
@@ -292,40 +297,44 @@
     )
     tail_copy.start()
     v = short(1, taps_v, 0)
-    mixed = gated(1, v)
-    asend[...] = jnp.concatenate(
-        [v.T.reshape(n, cpd, half), mixed.T.reshape(n, cpd, half)], axis=1).astype(BF16)
-    scatter(asend, arecv, a_sem)
-    arecv[seq] = asend[seq]
+    vsend[1] = v.T.reshape(n, cpd, half).astype(BF16)
+    scatter(vsend.at[1], vrecv.at[1], v_sem.at[1])
+    vrecv[1, seq] = vsend[1, seq]
+    msend[1] = gated(1, v).T.reshape(n, cpd, half).astype(BF16)
+    mrecv[1, seq] = msend[1, seq]
+
+    await_all(frecv, f_sem.at[1])
+    fwide[...] = frecv[...].astype(F32).reshape(n * 2 * cpd, half)
+    spectrum(rows_of(fwide, 0, 2 * cpd, fwide, cpd, 2 * cpd), spec_h)
 
     multiply(1, 1, left, both)
     multiply(1, 2, right, both)
     tail_copy.wait_recv()
     proj[pl.ds(0, HALO), :] = jnp.where(seq > 0, tail_in[...].astype(F32), 0.0)
     value_cols, gate_cols = pl.ds(0, cl), pl.ds(cl, cl)
-    for side in range(2):
-        from_far(1, side).wait_recv()
+    for p in range(1, len(pieces)):
+        for side in range(2):
+            from_far(p, side).wait_recv()
     multiply(1, 3, far, value_cols)
     finish(1, value_cols)
     v = short(0, taps_v, 0)
-    vsend[...] = v.T.reshape(n, cpd, half).astype(BF16)
-    scatter(vsend, vrecv, v_sem)
-    vrecv[seq] = vsend[seq]
+    vsend[0] = v.T.reshape(n, cpd, half).astype(BF16)
+    scatter(vsend.at[0], vrecv.at[0], v_sem.at[0])
+    vrecv[0, seq] = vsend[0, seq]
+    scatter(msend.at[1], mrecv.at[1], m_sem.at[1])
     multiply(1, 3, far, gate_cols)
     finish(1, gate_cols)
-    mixed = gated(0, v)
-    msend[...] = mixed.T.reshape(n, cpd, half).astype(BF16)
-    scatter(msend, mrecv, m_sem)
-    mrecv[seq] = msend[seq]
+    msend[0] = gated(0, v).T.reshape(n, cpd, half).astype(BF16)
+    scatter(msend.at[0], mrecv.at[0], m_sem.at[0])
+    mrecv[0, seq] = msend[0, seq]
     results = [local(0, gate, gate_ref), local(1, base, base_ref)]
     for c in results:
         c.start()
 
-    await_all(arecv, a_sem.at[1])
-    awide[...] = arecv[...].astype(F32).reshape(n * 2 * cpd, half)
-    await_all(vrecv, v_sem.at[1])
-    vwide[...] = vrecv[...].astype(F32).reshape(n * cpd, half)
-    spectrum(rows_of(vwide, 0, cpd, awide, 0, 2 * cpd), spec_v)
+    for h in (1, 0):
+        await_all(vrecv.at[h], v_sem.at[h, 1])
+        vwide[h] = vrecv[h].astype(F32).reshape(n * cpd, half)
+    spectrum(rows_of(vwide.at[0], 0, cpd, vwide.at[1], 0, cpd), spec_v)
     re, im = pl.ds(0, half), pl.ds(half, half)
     vr, vi = spec_v[:, re], spec_v[:, im]
     hr, hi = spec_h[:, re], spec_h[:, im]
@@ -334,9 +343,10 @@
     stays = [pltpu.make_async_copy(csend.at[seq], crecv.at[seq], own_sem.at[0])]
     stays[0].start()
 
-    await_all(mrecv, m_sem.at[1])
-    mwide[...] = mrecv[...].astype(F32).reshape(n * cpd, half)
-    spectrum(rows_of(mwide, 0, cpd, awide, cpd, 2 * cpd), spec_g)
+    for h in (1, 0):
+        await_all(mrecv.at[h], m_sem.at[h, 1])
+        vwide[h] = mrecv[h].astype(F32).reshape(n * cpd, half)
+    spectrum(rows_of(vwide.at[0], 0, cpd, vwide.at[1], 0, cpd), spec_g)
     gr, gi = spec_g[:, re], spec_g[:, im]
     vr, vi = spec_v[:, re], spec_v[:, im]
     restore(gr * vr + gi * vi, gi * vr - gr * vi, gsend)
@@ -344,12 +354,14 @@
     stays.append(pltpu.make_async_copy(gsend.at[seq], grecv.at[seq], own_sem.at[1]))
     stays[1].start()
 
-    for c in own[0] + own[1] + onward[0] + onward[1] + [tail_copy]:
+    for c in sum(own + onward, [tail_copy]):
         c.wait_send()
     for c in results + stays:
         c.wait()
-    for ref, sem in ((fsend, f_sem), (asend, a_sem), (vsend, v_sem), (msend, m_sem)):
-        await_all(ref, sem.at[0])
+    await_all(fsend, f_sem.at[0])
+    for h in range(2):
+        await_all(vsend.at[h], v_sem.at[h, 0])
+        await_all(msend.at[h], m_sem.at[h, 0])
     await_all(crecv, c_sem.at[1])
     await_all(csend, c_sem.at[0])
     await_all(grecv, g_sem.at[1])
@@ -398,33 +410,28 @@
         pltpu.VMEM((rows, cl), F32),
         pltpu.VMEM(block, BF16),
         pltpu.VMEM(block, BF16),
-        pltpu.VMEM(block, BF16),
-        pltpu.VMEM(block, BF16),
-        pltpu.VMEM(small, BF16),
-        pltpu.VMEM(small, BF16),
-        pltpu.VMEM(small, BF16),
-        pltpu.VMEM(small, BF16),
+        pltpu.VMEM((2, *small), BF16),
+        pltpu.VMEM((2, *small), BF16),
+        pltpu.VMEM((2, *small), BF16),
+        pltpu.VMEM((2, *small), BF16),
         pltpu.VMEM(block, BF16),
         pltpu.VMEM(block, BF16),
         pltpu.VMEM(block, F32),
         pltpu.VMEM((n * 2 * cpd, half), F32),
-        pltpu.VMEM((n * 2 * cpd, half), F32),
-        pltpu.VMEM((n * cpd, half), F32),
-        pltpu.VMEM((n * cpd, half), F32),
+        pltpu.VMEM((2, n * cpd, half), F32),
         pltpu.VMEM((cpd * count, 2 * half), BF16),
         pltpu.VMEM((cpd * count, 2 * half), F32),
         pltpu.VMEM((cpd * count, 2 * half), F32),
         pltpu.VMEM((cpd * count, 2 * half), F32),
         dma((11,)),
         dma((2 * yn,)),
-        dma((8,)),
-        dma((8,)),
+        dma((12,)),
+        dma((12,)),
         dma((2,)),
         dma((2,)),
         dma((2,)),
-        dma((2,)),
-        dma((2,)),
-        dma((2,)),
+        dma((2, 2)),
+        dma((2, 2)),
         dma((2,)),
         dma((2,)),
         pltpu.SemaphoreType.REGULAR((3,)),

time: 60.7 us -> 58.3 us (0.960)
  Pallas kernels: 59.9 us -> 57.6 us
    pallas_call x1, Pallas kernels: 57.6 us -> 55.3 us  [shards(): pl.pallas_call(functools.partial(transform_kernel, n, yn), out_shape=(jax...]
where the time goes in v3:
time: 58.3 us; the launch traced here: 58.2 us
  Pallas kernels  57.6 us (99%)
  between operations  0.64 us (1%)
    pallas_call x1, Pallas kernels, shards(): pl.pallas_call(functools.partial(transform_kernel, n, yn), out_shape=(jax...  55.3 us
    pallas_call x1, Pallas kernels, shards(): pl.pallas_call(closing_kernel, grid=(steps,), out_shape=(jax.ShapeDtypeSt...  2.31 us

profile of v3, /device:TPU:1, one launch (start us, length us, event | category | flops | bytes accessed | tf_op | source)
XLA Modules:
  0.0 58.2 jit_solution(14959026869707072798)
XLA Ops:
  0.6 55.3 %shard_map.140 = (bf16[64,16,128]{2,1,0:T(8,128)(2,1)}, bf16[64,16,128]{2,1,0:T(8,128)(2,1)}, f32[256,512]{1,0:T(8,128)}, f32[256,512]{1,0:T(8,128)}) custom-call(bf16[256,1024]{1,0:T(8,128)(2,1)} %tok_ref.1, bf16[4096,512]{1,0:T(8,128)(2,1)} %wv_ref.1, bf16[4096,512]{1,0:T(8,128)(2,1)} %wg_ref.1, f32[3,512]{1,0:T(4,128)} %taps_v_ref.1, ...), custom_call_target="tpu_custom_call" | custom-call | tf_op jit(solution)/shard_map/pallas_call | solution.py:439
  55.9 2.3 %shard_map.141 = (bf16[256,512]{1,0:T(8,128)(2,1)}, f32[256,512]{1,0:T(8,128)}) custom-call(bf16[64,16,128]{2,1,0:T(8,128)(2,1)} %get-tuple-element.6.conv_ref, bf16[64,16,128]{2,1,0:T(8,128)(2,1)} %get-tuple-element.7.grad_ref, f32[256,512]{1,0:T(8,128)} %get-tuple-element.8.gate_ref, f32[256,512]{1,0:T(8,128)} %get-tuple-element.9.base_ref), custom_call_target="tpu_custom_call" | custom-call | tf_op jit(solution)/shard_map/pallas_call | solution.py:457

commit v4 on v3

--- a/solution.py
+++ b/solution.py
@@ -46,10 +46,10 @@
     n, yn,
     tok_ref, wv_ref, wg_ref, taps_v_ref, taps_g_ref, skip_ref, filt_ref, gout_ref,
     first_ref, second_ref, third_ref, last_ref, twist_ref,
-    crecv, grecv, gate_ref, base_ref,
+    grecv, out_ref,
     tok, wall, taps_v, taps_g, skip, filt, gout, first, second, third, last, twist,
     acc, proj, tail, tail_in, gate, base,
-    fsend, frecv, vsend, vrecv, msend, mrecv, csend, gsend,
+    fsend, frecv, vsend, vrecv, msend, mrecv, csend, crecv, gsend, out,
     wide, fwide, vwide, mid, spec_v, spec_h, spec_g,
     loc_sem, w_sem, ag_send, ag_recv, tail_sem, own_sem,
     f_sem, v_sem, m_sem, c_sem, g_sem, met,
@@ -121,30 +121,40 @@
             device_id=device, device_id_type=MESH,
         )
 
-    own = [
-        [ag(4 * p, tok_ref.at[at], tok.at[ch, at], right_id),
-         ag(4 * p + 1, tok_ref.at[at], tok.at[ch, at], left_id)]
-        for p, at in enumerate(pieces)
-    ]
     low, high = pl.ds(0, dl // 2), pl.ds(dl // 2, dl // 2)
-
-    def forwards(p):
-        a, b = tok.at[left, pieces[p], low], tok.at[right, pieces[p], high]
-        return [ag(4 * p + 2, a, a, right_id), ag(4 * p + 3, b, b, left_id)]
-
-    onward = [forwards(p) for p in range(len(pieces))]
-
-    def from_neighbour(p, side):
-        src = (left, right)[side]
-        part = tok.at[src, pieces[p]]
-        return ag(4 * p + side, part, part, (right_id, left_id)[side])
+    ways = (right_id, left_id)
+
+    def own_part(p, kind):
+        cols = ((low, high), (high, low))[kind]
+        return [
+            ag(6 * p + 2 * kind + side, tok_ref.at[pieces[p], cols[side]], tok.at[ch, pieces[p], cols[side]], ways[side])
+            for side in range(2)
+        ]
+
+    def from_neighbour(p, kind, side):
+        part = tok.at[(left, right)[side], pieces[p], ((low, high), (high, low))[kind][side]]
+        return ag(6 * p + 2 * kind + side, part, part, ways[side])
 
     def from_far(p, side):
         part = tok.at[far, pieces[p], (low, high)[side]]
-        return ag(4 * p + 2 + side, part, part, (right_id, left_id)[side])
-
-    for c in own[0] + own[1]:
+        return ag(6 * p + 4 + side, part, part, ways[side])
+
+    own = [own_part(p, kind) for kind in range(2) for p in range(len(pieces))]
+    onward = []
+    for c in sum(own, []):
         c.start()
+
+    def pass_on(p):
+        for side in range(2):
+            from_neighbour(p, 0, side).wait_recv()
+            part = tok.at[(left, right)[side], pieces[p], (low, high)[side]]
+            c = ag(6 * p + 4 + side, part, part, ways[side])
+            c.start()
+            onward.append([c])
+
+    def rest(p):
+        for side in range(2):
+            from_neighbour(p, 1, side).wait_recv()
 
     def multiply(p, i, src, cols):
         part = dot(tok[src, spans[p], :], wall[pl.ds(pl.multiple_of(src * dl, dl), dl), cols])
@@ -212,12 +222,9 @@
     frecv[seq] = fsend[seq]
     multiply(1, 0, ch, both)
 
-    def pass_on(p):
-        for side in range(2):
-            from_neighbour(p, side).wait_recv()
-            onward[p][side].start()
-
-    pass_on(0)
+    for p in range(len(pieces)):
+        pass_on(p)
+    rest(0)
     for w in weights[1:3]:
         for c in w:
             c.wait()
@@ -281,9 +288,6 @@
         base[at, :] = g * skip[...] * v
         return gout[at, :].astype(F32) * g
 
-    for p in range(1, len(pieces)):
-        pass_on(p)
-
     for side in range(2):
         from_far(0, side).wait_recv()
     for c in weights[3]:
@@ -300,13 +304,13 @@
     vsend[1] = v.T.reshape(n, cpd, half).astype(BF16)
     scatter(vsend.at[1], vrecv.at[1], v_sem.at[1])
     vrecv[1, seq] = vsend[1, seq]
-    msend[1] = gated(1, v).T.reshape(n, cpd, half).astype(BF16)
-    mrecv[1, seq] = msend[1, seq]
+    wide[:, pl.ds(cpd, cpd), :] = gated(1, v).T.reshape(n, cpd, half)
 
     await_all(frecv, f_sem.at[1])
     fwide[...] = frecv[...].astype(F32).reshape(n * 2 * cpd, half)
     spectrum(rows_of(fwide, 0, 2 * cpd, fwide, cpd, 2 * cpd), spec_h)
 
+    rest(1)
     multiply(1, 1, left, both)
     multiply(1, 2, right, both)
     tail_copy.wait_recv()
@@ -321,15 +325,12 @@
     vsend[0] = v.T.reshape(n, cpd, half).astype(BF16)
     scatter(vsend.at[0], vrecv.at[0], v_sem.at[0])
     vrecv[0, seq] = vsend[0, seq]
-    scatter(msend.at[1], mrecv.at[1], m_sem.at[1])
     multiply(1, 3, far, gate_cols)
     finish(1, gate_cols)
-    msend[0] = gated(0, v).T.reshape(n, cpd, half).astype(BF16)
-    scatter(msend.at[0], mrecv.at[0], m_sem.at[0])
-    mrecv[0, seq] = msend[0, seq]
-    results = [local(0, gate, gate_ref), local(1, base, base_ref)]
-    for c in results:
-        c.start()
+    wide[:, pl.ds(0, cpd), :] = gated(0, v).T.reshape(n, cpd, half)
+    msend[...] = wide[...].astype(BF16)
+    scatter(msend, mrecv, m_sem)
+    mrecv[seq] = msend[seq]
 
     for h in (1, 0):
         await_all(vrecv.at[h], v_sem.at[h, 1])
@@ -340,46 +341,63 @@
     hr, hi = spec_h[:, re], spec_h[:, im]
     restore(vr * hr - vi * hi, vr * hi + vi * hr, csend)
     scatter(csend, crecv, c_sem)
-    stays = [pltpu.make_async_copy(csend.at[seq], crecv.at[seq], own_sem.at[0])]
-    stays[0].start()
-
-    for h in (1, 0):
-        await_all(mrecv.at[h], m_sem.at[h, 1])
-        vwide[h] = mrecv[h].astype(F32).reshape(n * cpd, half)
-    spectrum(rows_of(vwide.at[0], 0, cpd, vwide.at[1], 0, cpd), spec_g)
+    crecv[seq] = csend[seq]
+
+    await_all(mrecv, m_sem.at[1])
+    fwide[...] = mrecv[...].astype(F32).reshape(n * 2 * cpd, half)
+    spectrum(rows_of(fwide, 0, 2 * cpd, fwide, cpd, 2 * cpd), spec_g)
     gr, gi = spec_g[:, re], spec_g[:, im]
     vr, vi = spec_v[:, re], spec_v[:, im]
     restore(gr * vr + gi * vi, gi * vr - gr * vi, gsend)
     scatter(gsend, grecv, g_sem)
-    stays.append(pltpu.make_async_copy(gsend.at[seq], grecv.at[seq], own_sem.at[1]))
-    stays[1].start()
+    stays = pltpu.make_async_copy(gsend.at[seq], grecv.at[seq], own_sem.at[0])
+    stays.start()
+
+    await_all(crecv, c_sem.at[1])
+    wide[...] = crecv[...].astype(F32)
+    for h in range(2):
+        at = pl.ds(h * half, half)
+        y = wide[:, pl.ds(h * cpd, cpd), :].reshape(cl, half).T
+        out[at, :] = (gate[at, :] * y + base[at, :]).astype(BF16)
+    result = pltpu.make_async_copy(out, out_ref, own_sem.at[1])
+    result.start()
 
     for c in sum(own + onward, [tail_copy]):
         c.wait_send()
-    for c in results + stays:
-        c.wait()
+    stays.wait()
+    result.wait()
     await_all(fsend, f_sem.at[0])
+    await_all(msend, m_sem.at[0])
     for h in range(2):
         await_all(vsend.at[h], v_sem.at[h, 0])
-        await_all(msend.at[h], m_sem.at[h, 0])
-    await_all(crecv, c_sem.at[1])
     await_all(csend, c_sem.at[0])
     await_all(grecv, g_sem.at[1])
     await_all(gsend, g_sem.at[0])
 
 
-def closing_kernel(conv_ref, grad_ref, gate_ref, base_ref, out_ref, fgrad_ref):
-    cpd = conv_ref.shape[1] // 2
-    half = conv_ref.shape[2]
-    columns = out_ref.shape[1]
-
-    def turned(ref, h):
-        return ref[...].astype(F32)[:, h * cpd:(h + 1) * cpd, :].reshape(columns, half).T
-
-    for h in range(2):
-        at = pl.ds(h * half, half)
-        out_ref[at, :] = (gate_ref[at, :] * turned(conv_ref, h) + base_ref[at, :]).astype(BF16)
-        fgrad_ref[at, :] = turned(grad_ref, h)
+def closing_kernel(steps, grad_ref, out_in_ref, out_ref, fgrad_ref, grad, fgrad, sem):
+    cpd = grad_ref.shape[1] // 2
+    half = grad_ref.shape[2]
+    blocks = grad_ref.shape[0] // steps
+    columns = fgrad_ref.shape[1] // steps
+    moved = pltpu.make_async_copy(out_in_ref, out_ref, sem.at[0])
+    arrive, leave = [], []
+    for i in range(steps):
+        at, cols = pl.ds(i * blocks, blocks), pl.ds(i * columns, columns)
+        arrive.append(pltpu.make_async_copy(grad_ref.at[at], grad.at[at], sem.at[1 + 2 * i]))
+        leave.append(pltpu.make_async_copy(fgrad.at[:, cols], fgrad_ref.at[:, cols], sem.at[2 + 2 * i]))
+    for c in arrive:
+        c.start()
+    moved.start()
+    for i in range(steps):
+        arrive[i].wait()
+        x = grad[pl.ds(i * blocks, blocks)].astype(F32)
+        for h in range(2):
+            fgrad[pl.ds(h * half, half), pl.ds(i * columns, columns)] = (
+                x[:, h * cpd:(h + 1) * cpd, :].reshape(columns, half).T)
+        leave[i].start()
+    for c in leave + [moved]:
+        c.wait()
 
 
 def shards(n, yn, tokens, w_value, w_gate, short_value, short_gate, skip_bias, long_filter, grad_out):
@@ -412,10 +430,12 @@
         pltpu.VMEM(block, BF16),
         pltpu.VMEM((2, *small), BF16),
         pltpu.VMEM((2, *small), BF16),
-        pltpu.VMEM((2, *small), BF16),
-        pltpu.VMEM((2, *small), BF16),
-        pltpu.VMEM(block, BF16),
-        pltpu.VMEM(block, BF16),
+        pltpu.VMEM(block, BF16),
+        pltpu.VMEM(block, BF16),
+        pltpu.VMEM(block, BF16),
+        pltpu.VMEM(block, BF16),
+        pltpu.VMEM(block, BF16),
+        pltpu.VMEM((rows, cl), BF16),
         pltpu.VMEM(block, F32),
         pltpu.VMEM((n * 2 * cpd, half), F32),
         pltpu.VMEM((2, n * cpd, half), F32),
@@ -431,39 +451,35 @@
         dma((2,)),
         dma((2,)),
         dma((2, 2)),
-        dma((2, 2)),
+        dma((2,)),
         dma((2,)),
         dma((2,)),
         pltpu.SemaphoreType.REGULAR((3,)),
     ]
-    conv, grad, gate, base = pl.pallas_call(
+    grad, out = pl.pallas_call(
         functools.partial(transform_kernel, n, yn),
         out_shape=(
             jax.ShapeDtypeStruct(block, BF16),
-            jax.ShapeDtypeStruct(block, BF16),
-            jax.ShapeDtypeStruct((rows, cl), F32),
-            jax.ShapeDtypeStruct((rows, cl), F32),
+            jax.ShapeDtypeStruct((rows, cl), BF16),
         ),
         in_specs=[anywhere] * 13,
-        out_specs=[anywhere] * 4,
+        out_specs=[anywhere] * 2,
         scratch_shapes=scratch,
         compiler_params=pltpu.CompilerParams(
             collective_id=0, has_side_effects=True, vmem_limit_bytes=56 * 1024 * 1024
         ),
     )(tokens, w_value, w_gate, short_value, short_gate, skip_bias[None], long_filter, grad_out, *consts)
-    steps = 2
-    blocks = pl.BlockSpec((n // steps, 2 * cpd, half), lambda i: (i, 0, 0))
-    columns = pl.BlockSpec((rows, cl // steps), lambda i: (0, i))
+    steps = 4 if cl % 512 == 0 else 1
     return pl.pallas_call(
-        closing_kernel,
-        grid=(steps,),
+        functools.partial(closing_kernel, steps),
         out_shape=(
             jax.ShapeDtypeStruct((rows, cl), BF16),
             jax.ShapeDtypeStruct((rows, cl), F32),
         ),
-        in_specs=[blocks, blocks, columns, columns],
-        out_specs=(columns, columns),
-    )(conv, grad, gate, base)
+        in_specs=[anywhere] * 2,
+        out_specs=[anywhere] * 2,
+        scratch_shapes=[pltpu.VMEM(block, BF16), pltpu.VMEM((rows, cl), F32), dma((1 + 2 * steps,))],
+    )(grad, out)
 
 
 def solution(mesh):

time: 58.3 us -> 65.5 us (1.12)
  Pallas kernels: 57.6 us -> 64.7 us
    pallas_call x1, Pallas kernels: 2.31 us -> 9.13 us  [shards(): pl.pallas_call(functools.partial(closing_kernel, steps), out_shape=(jax.S...]
where the time goes in v4:
time: 65.5 us; the launch traced here: 65.4 us
  Pallas kernels  64.7 us (99%)
    pallas_call x1, Pallas kernels, shards(): pl.pallas_call(functools.partial(transform_kernel, n, yn), out_shape=(jax...  55.6 us
    pallas_call x1, Pallas kernels, shards(): pl.pallas_call(functools.partial(closing_kernel, steps), out_shape=(jax.S...  9.13 us

profile of v4, /device:TPU:1, one launch (start us, length us, event | category | flops | bytes accessed | tf_op | source)
XLA Modules:
  0.0 65.4 jit_solution(17105763321252316928)
XLA Ops:
  0.6 55.6 %shard_map.140 = (bf16[64,16,128]{2,1,0:T(8,128)(2,1)}, bf16[256,512]{1,0:T(8,128)(2,1)}) custom-call(bf16[256,1024]{1,0:T(8,128)(2,1)} %tok_ref.1, bf16[4096,512]{1,0:T(8,128)(2,1)} %wv_ref.1, bf16[4096,512]{1,0:T(8,128)(2,1)} %wg_ref.1, f32[3,512]{1,0:T(4,128)} %taps_v_ref.1, f32[3,512]{1,0:T(4,128)} %taps_g_ref.1, f32[1,512]{1,0:T(1,128)} %bitcast.1, ...), custom_call_target="tpu_custom_call" | custom-call | tf_op jit(solution)/shard_map/pallas_call | solution.py:459
  56.2 9.1 %shard_map.141 = (bf16[256,512]{1,0:T(8,128)(2,1)}, f32[256,512]{1,0:T(8,128)}) custom-call(bf16[64,16,128]{2,1,0:T(8,128)(2,1)} %get-tuple-element.4.grad_ref, bf16[256,512]{1,0:T(8,128)(2,1)} %get-tuple-element.5.out_in_ref), custom_call_target="tpu_custom_call" | custom-call | tf_op jit(solution)/shard_map/pallas_call | solution.py:473

commit v5 on v4

--- a/solution.py
+++ b/solution.py
@@ -306,10 +306,6 @@
     vrecv[1, seq] = vsend[1, seq]
     wide[:, pl.ds(cpd, cpd), :] = gated(1, v).T.reshape(n, cpd, half)
 
-    await_all(frecv, f_sem.at[1])
-    fwide[...] = frecv[...].astype(F32).reshape(n * 2 * cpd, half)
-    spectrum(rows_of(fwide, 0, 2 * cpd, fwide, cpd, 2 * cpd), spec_h)
-
     rest(1)
     multiply(1, 1, left, both)
     multiply(1, 2, right, both)
@@ -329,6 +325,9 @@
     finish(1, gate_cols)
     wide[:, pl.ds(0, cpd), :] = gated(0, v).T.reshape(n, cpd, half)
     msend[...] = wide[...].astype(BF16)
+    await_all(frecv, f_sem.at[1])
+    fwide[...] = frecv[...].astype(F32).reshape(n * 2 * cpd, half)
+    spectrum(rows_of(fwide, 0, 2 * cpd, fwide, cpd, 2 * cpd), spec_h)
     scatter(msend, mrecv, m_sem)
     mrecv[seq] = msend[seq]
 
@@ -375,29 +374,14 @@
     await_all(gsend, g_sem.at[0])
 
 
-def closing_kernel(steps, grad_ref, out_in_ref, out_ref, fgrad_ref, grad, fgrad, sem):
+def closing_kernel(grad_ref, out_in_ref, out_ref, fgrad_ref):
     cpd = grad_ref.shape[1] // 2
     half = grad_ref.shape[2]
-    blocks = grad_ref.shape[0] // steps
-    columns = fgrad_ref.shape[1] // steps
-    moved = pltpu.make_async_copy(out_in_ref, out_ref, sem.at[0])
-    arrive, leave = [], []
-    for i in range(steps):
-        at, cols = pl.ds(i * blocks, blocks), pl.ds(i * columns, columns)
-        arrive.append(pltpu.make_async_copy(grad_ref.at[at], grad.at[at], sem.at[1 + 2 * i]))
-        leave.append(pltpu.make_async_copy(fgrad.at[:, cols], fgrad_ref.at[:, cols], sem.at[2 + 2 * i]))
-    for c in arrive:
-        c.start()
-    moved.start()
-    for i in range(steps):
-        arrive[i].wait()
-        x = grad[pl.ds(i * blocks, blocks)].astype(F32)
-        for h in range(2):
-            fgrad[pl.ds(h * half, half), pl.ds(i * columns, columns)] = (
-                x[:, h * cpd:(h + 1) * cpd, :].reshape(columns, half).T)
-        leave[i].start()
-    for c in leave + [moved]:
-        c.wait()
+    columns = out_ref.shape[1]
+    out_ref[...] = out_in_ref[...]
+    x = grad_ref[...].astype(F32)
+    for h in range(2):
+        fgrad_ref[pl.ds(h * half, half), :] = x[:, h * cpd:(h + 1) * cpd, :].reshape(columns, half).T
 
 
 def shards(n, yn, tokens, w_value, w_gate, short_value, short_gate, skip_bias, long_filter, grad_out):
@@ -469,16 +453,18 @@
             collective_id=0, has_side_effects=True, vmem_limit_bytes=56 * 1024 * 1024
         ),
     )(tokens, w_value, w_gate, short_value, short_gate, skip_bias[None], long_filter, grad_out, *consts)
-    steps = 4 if cl % 512 == 0 else 1
+    steps = 2
+    blocks = pl.BlockSpec((n // steps, 2 * cpd, half), lambda i: (i, 0, 0))
+    columns = pl.BlockSpec((rows, cl // steps), lambda i: (0, i))
     return pl.pallas_call(
-        functools.partial(closing_kernel, steps),
+        closing_kernel,
+        grid=(steps,),
         out_shape=(
             jax.ShapeDtypeStruct((rows, cl), BF16),
             jax.ShapeDtypeStruct((rows, cl), F32),
         ),
-        in_specs=[anywhere] * 2,
-        out_specs=[anywhere] * 2,
-        scratch_shapes=[pltpu.VMEM(block, BF16), pltpu.VMEM((rows, cl), F32), dma((1 + 2 * steps,))],
+        in_specs=[blocks, columns],
+        out_specs=(columns, columns),
     )(grad, out)
 
 

time: 65.5 us -> 57.8 us (0.88)
  Pallas kernels: 64.7 us -> 57.1 us
    pallas_call x1, Pallas kernels: 9.13 us -> 1.92 us  [shards(): pl.pallas_call(closing_kernel, grid=(steps,), out_shape=(jax.ShapeDtypeSt...]
where the time goes in v5:
time: 57.8 us; the launch traced here: 57.7 us
  Pallas kernels  57.1 us (99%)
  between operations  0.64 us (1%)
    pallas_call x1, Pallas kernels, shards(): pl.pallas_call(functools.partial(transform_kernel, n, yn), out_shape=(jax...  55.2 us
    pallas_call x1, Pallas kernels, shards(): pl.pallas_call(closing_kernel, grid=(steps,), out_shape=(jax.ShapeDtypeSt...  1.92 us

profile of v5, /device:TPU:1, one launch (start us, length us, event | category | flops | bytes accessed | tf_op | source)
XLA Modules:
  0.0 57.7 jit_solution(2277741332968630536)
XLA Ops:
  0.6 55.2 %shard_map.140 = (bf16[64,16,128]{2,1,0:T(8,128)(2,1)}, bf16[256,512]{1,0:T(8,128)(2,1)}) custom-call(bf16[256,1024]{1,0:T(8,128)(2,1)} %tok_ref.1, bf16[4096,512]{1,0:T(8,128)(2,1)} %wv_ref.1, bf16[4096,512]{1,0:T(8,128)(2,1)} %wg_ref.1, f32[3,512]{1,0:T(4,128)} %taps_v_ref.1, f32[3,512]{1,0:T(4,128)} %taps_g_ref.1, f32[1,512]{1,0:T(1,128)} %bitcast.1, ...), custom_call_target="tpu_custom_call" | custom-call | tf_op jit(solution)/shard_map/pallas_call | solution.py:443
  55.8 1.9 %shard_map.141 = (bf16[256,512]{1,0:T(8,128)(2,1)}, f32[256,512]{1,0:T(8,128)}) custom-call(bf16[64,16,128]{2,1,0:T(8,128)(2,1)} %get-tuple-element.4.grad_ref, bf16[256,512]{1,0:T(8,128)(2,1)} %get-tuple-element.5.out_in_ref), custom_call_target="tpu_custom_call" | custom-call | tf_op jit(solution)/shard_map/pallas_call | solution.py:459

commit v6 on v5

--- a/solution.py
+++ b/solution.py
@@ -139,7 +139,8 @@
         part = tok.at[far, pieces[p], (low, high)[side]]
         return ag(6 * p + 4 + side, part, part, ways[side])
 
-    own = [own_part(p, kind) for kind in range(2) for p in range(len(pieces))]
+    own = [own_part(0, 0), own_part(0, 1), own_part(1, 0)]
+    delayed = own_part(1, 1)
     onward = []
     for c in sum(own, []):
         c.start()
@@ -222,8 +223,11 @@
     frecv[seq] = fsend[seq]
     multiply(1, 0, ch, both)
 
-    for p in range(len(pieces)):
-        pass_on(p)
+    pass_on(0)
+    for c in delayed:
+        c.start()
+    own.append(delayed)
+    pass_on(1)
     rest(0)
     for w in weights[1:3]:
         for c in w:

time: 57.8 us -> 56.3 us (0.974)
  Pallas kernels: 57.1 us -> 55.6 us
    pallas_call x1, Pallas kernels: 55.2 us -> 53.6 us  [shards(): pl.pallas_call(functools.partial(transform_kernel, n, yn), out_shape=(jax...]
where the time goes in v6:
time: 56.3 us; the launch traced here: 56.2 us
  Pallas kernels  55.6 us (99%)
  between operations  0.64 us (1%)
    pallas_call x1, Pallas kernels, shards(): pl.pallas_call(functools.partial(transform_kernel, n, yn), out_shape=(jax...  53.6 us
    pallas_call x1, Pallas kernels, shards(): pl.pallas_call(closing_kernel, grid=(steps,), out_shape=(jax.ShapeDtypeSt...  1.92 us

profile of v6, /device:TPU:1, one launch (start us, length us, event | category | flops | bytes accessed | tf_op | source)
XLA Modules:
  0.0 56.2 jit_solution(14262093357019200765)
XLA Ops:
  0.6 53.6 %shard_map.140 = (bf16[64,16,128]{2,1,0:T(8,128)(2,1)}, bf16[256,512]{1,0:T(8,128)(2,1)}) custom-call(bf16[256,1024]{1,0:T(8,128)(2,1)} %tok_ref.1, bf16[4096,512]{1,0:T(8,128)(2,1)} %wv_ref.1, bf16[4096,512]{1,0:T(8,128)(2,1)} %wg_ref.1, f32[3,512]{1,0:T(4,128)} %taps_v_ref.1, f32[3,512]{1,0:T(4,128)} %taps_g_ref.1, f32[1,512]{1,0:T(1,128)} %bitcast.1, ...), custom_call_target="tpu_custom_call" | custom-call | tf_op jit(solution)/shard_map/pallas_call | solution.py:447
  54.3 1.9 %shard_map.141 = (bf16[256,512]{1,0:T(8,128)(2,1)}, f32[256,512]{1,0:T(8,128)}) custom-call(bf16[64,16,128]{2,1,0:T(8,128)(2,1)} %get-tuple-element.4.grad_ref, bf16[256,512]{1,0:T(8,128)(2,1)} %get-tuple-element.5.out_in_ref), custom_call_target="tpu_custom_call" | custom-call | tf_op jit(solution)/shard_map/pallas_call | solution.py:463

commit v7 on v6

--- a/solution.py
+++ b/solution.py
@@ -224,10 +224,10 @@
     multiply(1, 0, ch, both)
 
     pass_on(0)
+    pass_on(1)
     for c in delayed:
         c.start()
     own.append(delayed)
-    pass_on(1)
     rest(0)
     for w in weights[1:3]:
         for c in w:

time: 56.3 us -> 57.1 us (1.014)
  Pallas kernels: 55.6 us -> 56.3 us
    pallas_call x1, Pallas kernels: 53.6 us -> 54.4 us  [shards(): pl.pallas_call(functools.partial(transform_kernel, n, yn), out_shape=(jax...]
where the time goes in v7:
time: 57.1 us; the launch traced here: 57 us
  Pallas kernels  56.3 us (99%)
  between operations  0.64 us (1%)
    pallas_call x1, Pallas kernels, shards(): pl.pallas_call(functools.partial(transform_kernel, n, yn), out_shape=(jax...  54.4 us
    pallas_call x1, Pallas kernels, shards(): pl.pallas_call(closing_kernel, grid=(steps,), out_shape=(jax.ShapeDtypeSt...  1.92 us

profile of v7, /device:TPU:1, one launch (start us, length us, event | category | flops | bytes accessed | tf_op | source)
XLA Modules:
  0.0 57.0 jit_solution(15214794042359796449)
XLA Ops:
  0.6 54.4 %shard_map.140 = (bf16[64,16,128]{2,1,0:T(8,128)(2,1)}, bf16[256,512]{1,0:T(8,128)(2,1)}) custom-call(bf16[256,1024]{1,0:T(8,128)(2,1)} %tok_ref.1, bf16[4096,512]{1,0:T(8,128)(2,1)} %wv_ref.1, bf16[4096,512]{1,0:T(8,128)(2,1)} %wg_ref.1, f32[3,512]{1,0:T(4,128)} %taps_v_ref.1, f32[3,512]{1,0:T(4,128)} %taps_g_ref.1, f32[1,512]{1,0:T(1,128)} %bitcast.1, ...), custom_call_target="tpu_custom_call" | custom-call | tf_op jit(solution)/shard_map/pallas_call | solution.py:447
  55.0 1.9 %shard_map.141 = (bf16[256,512]{1,0:T(8,128)(2,1)}, f32[256,512]{1,0:T(8,128)}) custom-call(bf16[64,16,128]{2,1,0:T(8,128)(2,1)} %get-tuple-element.4.grad_ref, bf16[256,512]{1,0:T(8,128)(2,1)} %get-tuple-element.5.out_in_ref), custom_call_target="tpu_custom_call" | custom-call | tf_op jit(solution)/shard_map/pallas_call | solution.py:463
